TPU v7x, 128 devices: a whole 4x4x4 slice. The times are simulated.
128 devices in a mesh: row: 16 (over z_hi, y, core), col: 8 (over x, z_lo).
Axes of the slice: x: 4, y: 4, z: 4 (z_hi: 2, z_lo: 2; z = z_hi * 2 + z_lo), core: 2. Of those that a mesh axis runs over, the one named last changes fastest.
Arguments:
- inputs: bfloat16 [4, 65536, 1024], P(None, ('row', 'col')), may hold values from -36 to 36
- cotangents: bfloat16 [4, 65536, 1024], P(None, ('row', 'col')), may hold values from -0.5745243 to 0.5745243
- error_buffer: bfloat16 [128, 4, 1024, 1024], P(('row', 'col')), may hold values from -24 to 24
- previous_q: float32 [4, 32, 1024], replicated, may hold values from -6 to 6
Outputs:
- new_error: bfloat16 [128, 4, 1024, 1024], P(('row', 'col'))
- update: bfloat16 [4, 1024, 1024], P(None, ('row', 'col'))
- new_q: float32 [4, 32, 1024], replicated
All inputs are finite; a program needn't handle non-finite values.
Results may differ from a plain program's by a relative error of at most 0.001.
Values sent between devices are 32-bit elements; how exact they have to be, the bound alone decides.
No kernel may reach another device: no remote copies, remote signals or barrier semaphores. Data moves between devices by JAX's collectives and lax.ppermute only.
A program may use at most 128 MiB of HBM per device.

v0:
```python
import jax
import jax.numpy as jnp
from jax import lax
from jax.sharding import PartitionSpec as P


def gram_schmidt(p_rows):
    finished = []
    for column in range(p_rows.shape[1]):
        vector = p_rows[:, column, :]
        for earlier in finished:
            vector = vector - jnp.sum(earlier * vector, axis=-1, keepdims=True) * earlier
        vector = vector / jnp.sqrt(jnp.sum(vector * vector, axis=-1, keepdims=True) + 1e-06)
        finished.append(vector)
    return jnp.stack(finished, axis=1)


def on_device(inputs, cotangents, error_buffer, previous_q):
    highest = lax.Precision.HIGHEST
    devices = lax.axis_size(("row", "col"))
    grads = jnp.einsum("mti,mtj->mij", inputs, cotangents, preferred_element_type=jnp.float32)
    merged = grads + error_buffer[0].astype(jnp.float32)
    local_p = jnp.einsum("mrj,mij->mri", previous_q, merged, precision=highest)
    summed = lax.psum(local_p, ("row", "col")) / devices
    basis = gram_schmidt(summed)
    local_q = jnp.einsum("mri,mij->mrj", basis, merged, precision=highest)
    new_q = lax.psum(local_q, ("row", "col")) / devices
    decompressed = jnp.einsum("mri,mrj->mij", basis, new_q, precision=highest)
    new_error = (merged - decompressed).astype(jnp.bfloat16)[None]
    row_count = decompressed.shape[1] // devices
    first_row = lax.axis_index(("row", "col")) * row_count
    own_rows = lax.dynamic_slice_in_dim(decompressed, first_row, row_count, 1).astype(jnp.bfloat16)
    return (new_error, own_rows, new_q)


def solution(mesh):
    return jax.shard_map(
        on_device,
        mesh=mesh,
        in_specs=(
            P(None, ("row", "col"), None),
            P(None, ("row", "col"), None),
            P(("row", "col"), None, None, None),
            P(),
        ),
        out_specs=(P(("row", "col"), None, None, None), P(None, ("row", "col"), None), P()),
        check_vma=False,
    )
```

profile of v0, /device:TPU:1, one launch (start us, length us, event | category | flops | bytes accessed | tf_op | source)
XLA Modules:
  0.0 456.2 jit_solution(14436774694549399703)
XLA Ops:
  7.2 16.2 %convert_add_fusion = f32[4,1024,1024]{2,1,0:T(8,128)} fusion(bf16[4,512,1024]{2,1,0:T(8,128)(2,1)} %param.4, bf16[4,512,1024]{2,1,0:T(8,128)(2,1)} %param.5, bf16[1,4,1024,1024]{3,2,1,0:T(8,128)(2,1)} %param.6), kind=kOutput, calls=%fused_computation | convolution fusion | flops 4303355904 | bytes 33554432 | tf_op jit(solution)/shard_map/mti,mtj->mij/dot_general | solution.py:21
  23.4 18.9 %fusion.37 = f32[4,1024,32]{1,2,0:T(8,128)S(1)} fusion(f32[4,1024,1024]{2,1,0:T(8,128)} %convert_add_fusion, f32[4,32,1024]{2,1,0:T(8,128)S(1)} %copy-done), kind=kOutput, calls=%fused_computation.1192 | convolution fusion | flops 1610612736 | bytes 17825792 | tf_op jit(solution)/shard_map/mrj,mij->mri/dot_general | solution.py:23
  42.3 1.1 copy.487
  43.7 148.4 %all-reduce.3.cloned.1.call-done = f32[4,32,1024]{2,0,1:T(4,128)} async-done(((f32[4,32,1024]{2,0,1:T(4,128)}), f32[4,32,1024]{2,0,1:T(4,128)}) %all-reduce.3.cloned.1.call-update) | async-done | bytes 524304 | tf_op jit(solution)/shard_map/psum | solution.py:24
  192.1 1.2 broadcast_multiply_fusion.1
  199.7 0.6 multiply_reduce_fusion.26
  202.2 0.6 multiply_reduce_fusion.24
  206.7 0.6 multiply_reduce_fusion.20
  212.3 0.7 subtract_divide_fusion.19
  225.0 0.6 constant_dynamic-update-slice_fusion.15
  225.6 0.7 constant_dynamic-update-slice_fusion.14
  226.4 0.8 constant_dynamic-update-slice_fusion.13
  227.2 0.9 constant_dynamic-update-slice_fusion.12
  228.1 1.0 constant_dynamic-update-slice_fusion.11
  229.1 1.1 constant_dynamic-update-slice_fusion.10
  230.2 3.6 constant_dynamic-update-slice_fusion.9
  233.8 3.9 constant_dynamic-update-slice_fusion.8
  237.7 4.3 constant_dynamic-update-slice_fusion.7
  242.1 3.8 constant_dynamic-update-slice_fusion.6
  245.9 3.8 constant_dynamic-update-slice_fusion.5
  249.7 3.5 constant_dynamic-update-slice_fusion.4
  253.2 1.1 constant_dynamic-update-slice_fusion.3
  254.3 1.1 constant_dynamic-update-slice_fusion.2
  255.3 4.4 constant_dynamic-update-slice_fusion.1
  259.7 4.8 %constant_dynamic-update-slice_fusion = f32[4,32,1024]{2,0,1:T(4,128)S(1)} fusion(f32[4,32,1024]{2,0,1:T(4,128)S(1)} %get-tuple-element.835, f32[4,1,1024]{2,0,1:T(4,128)S(1)} %get-tuple-element.510, f32[4,1,1024]{2,0,1:T(4,128)S(1)} %get-tuple-element.515, f32[4,1,1024]{2,0,1:T(4,128)S(1)} %get-tuple-element.523, f32[4,1,1024]{2,0,1:T(4,128)S(1)} %get-tuple-element.834, ...), kind=kLoop, calls=%fused_computation.11 | loop fusion | flops 2723840 | bytes 843776 | tf_op jit(solution)/shard_map/stack | solution.py:15
  264.5 13.4 %fusion.1 = f32[4,32,1024]{2,1,0:T(8,128)S(1)} fusion(f32[4,1024,1024]{2,1,0:T(8,128)} %convert_add_fusion, f32[4,32,1024]{2,0,1:T(4,128)S(1)} %constant_dynamic-update-slice_fusion), kind=kOutput, calls=%fused_computation.4 | convolution fusion | flops 1610612736 | bytes 17825792 | tf_op jit(solution)/shard_map/mri,mij->mrj/dot_general | solution.py:26
  277.9 1.1 copy.477
  279.1 143.9 %all-reduce.5.cloned.1.call-done = f32[4,32,1024]{2,0,1:T(4,128)} async-done(((f32[4,32,1024]{2,0,1:T(4,128)}), f32[4,32,1024]{2,0,1:T(4,128)}) %all-reduce.5.cloned.1.call-update) | async-done | bytes 524304 | tf_op jit(solution)/shard_map/psum | solution.py:27
  423.0 1.2 broadcast_multiply_fusion
  424.5 13.8 %fusion.3 = f32[4,1024,1024]{2,1,0:T(8,128)S(1)} fusion(f32[4,32,1024]{2,1,0:T(8,128)S(1)} %copy.479, f32[4,32,1024]{2,0,1:T(4,128)S(1)} %constant_dynamic-update-slice_fusion), kind=kOutput, calls=%fused_computation.6 | convolution fusion | flops 1610612736 | bytes 17825792 | tf_op jit(solution)/shard_map/mri,mrj->mij/dot_general | solution.py:28
  438.3 9.9 %fusion = bf16[1,4,1024,1024]{3,2,1,0:T(8,128)(2,1)} fusion(f32[4,1024,1024]{2,1,0:T(8,128)} %convert_add_fusion, f32[4,1024,1024]{2,1,0:T(8,128)S(1)} %fusion.3), kind=kLoop, calls=%fused_computation.2 | loop fusion | flops 8388608 | bytes 41943040 | tf_op jit(solution)/shard_map/broadcast_in_dim | solution.py:29
  448.3 0.6 dynamic-slice_convert_fusion
  (151 shorter events, 29.7 us)
Async XLA Ops:
  7.2 16.2 %copy-start = (f32[4,32,1024]{2,1,0:T(8,128)S(1)}, f32[4,32,1024]{2,1,0:T(8,128)}, u32[]{:S(2)}) copy-start(f32[4,32,1024]{2,1,0:T(8,128)} %param.7) | copy-start | bytes 1572868
  7.2 184.9 %all-reduce.3.cloned.1.call-start = ((), (), s32[]{:S(2)}) async-start(), calls=%async_computation | async-start | bytes 1048576 | tf_op jit(solution)/shard_map/psum | solution.py:24
  43.4 379.6 %all-reduce.5.cloned.1.call-start = ((), (), s32[]{:S(2)}) async-start(), calls=%async_computation.1 | async-start | bytes 1048576 | tf_op jit(solution)/shard_map/psum | solution.py:27
  424.5 23.8 %copy-start.2 = (f32[4,32,1024]{2,1,0:T(8,128)}, f32[4,32,1024]{2,1,0:T(8,128)S(1)}, u32[]{:S(2)}) copy-start(f32[4,32,1024]{2,1,0:T(8,128)S(1)} %copy.479) | copy-start | bytes 1572868
  424.5 24.4 %copy-start.1 = (f32[4,32,1024]{2,1,0:T(8,128)S(1)}, f32[4,32,1024]{2,1,0:T(8,128)}, u32[]{:S(2)}) copy-start(f32[4,32,1024]{2,1,0:T(8,128)} %param.7) | copy-start | bytes 1572868
Sparse Core Ops, SparseCore 0:
  43.6 148.4 all-reduce.2
  279.2 143.7 all-reduce.4
where the time goes:
time: 464 us; the launch traced here: 456 us
  waiting for transfers between devices  292 us (63%)
  other arithmetic  83.1 us (18%)
  matrix products  62.2 us (13%)
  between operations  14.9 us (3%)
    psum x1, waiting for transfers between devices, on_device(): summed = lax.psum(local_p, ('row', 'col')) / devices  148 us
    psum x1, waiting for transfers between devices, on_device(): new_q = lax.psum(local_q, ('row', 'col')) / devices  144 us
    unnamed x25, other arithmetic  37.4 us
    reduce_sum x74, other arithmetic, gram_schmidt(): jnp.sum(earlier * vector, axis=-1, keepdims=True) * earlier  23.4 us
    dot_general x1, matrix products, on_device(): local_p = jnp.einsum('mrj,mij->mri', previous_q, merged, precision=highest)  18.9 us
    dot_general x1, matrix products, on_device(): jnp.einsum('mti,mtj->mij', inputs, cotangents, preferred_element_type=jnp...  16.2 us
    dot_general x1, matrix products, on_device(): decompressed = jnp.einsum('mri,mrj->mij', basis, new_q, precision=highest)  13.8 us
    dot_general x1, matrix products, on_device(): local_q = jnp.einsum('mri,mij->mrj', basis, merged, precision=highest)  13.4 us
  transfers between devices with their start and end apart: 2, of which 2 were waited for; matrix products, arithmetic and copies ran while one was open for 0% of the time, Pallas kernels for 0%

commit v1 on v0

v1 whole, which is shorter than its diff:
```python
import jax
import jax.numpy as jnp
from jax import lax
from jax.experimental import pallas as pl
from jax.experimental.pallas import tpu as pltpu
from jax.sharding import PartitionSpec as P

AXES = ("row", "col")
SIZES = (("zh", 2), ("y", 4), ("core", 2), ("x", 4), ("zl", 2))
MATCHINGS = (("x", 0), ("y", 0), ("z", 0), ("x", 1), ("y", 1), ("z", 1))
FIRST = ((0, 3), (1, 4))


def coords_of(index):
    coords = {}
    for name, size in reversed(SIZES):
        coords[name] = index % size
        index //= size
    return coords


def index_of(coords):
    index = 0
    for name, size in SIZES:
        index = index * size + coords[name]
    return index


def partner(index, matching):
    coords = coords_of(index)
    axis, odd = matching
    if axis == "z":
        z = 2 * coords["zh"] + coords["zl"]
        z = 3 - z if odd else z ^ 1
        coords["zh"], coords["zl"] = z // 2, z % 2
    else:
        coords[axis] = 3 - coords[axis] if odd else coords[axis] ^ 1
    return index_of(coords)


def step_pairs(flow, step):
    pairs = []
    for index in range(128):
        first = FIRST[flow][coords_of(index)["core"]]
        pairs.append((index, partner(index, MATCHINGS[(first + step) % 6])))
    return pairs


def core_pairs():
    pairs = []
    for index in range(128):
        coords = coords_of(index)
        coords["core"] ^= 1
        pairs.append((index, index_of(coords)))
    return pairs


def other_core(value):
    return lax.ppermute(value, AXES, core_pairs())


MIB = 1024 * 1024
VMEM = pl.BlockSpec(memory_space=pltpu.VMEM)
HBM = pl.BlockSpec(memory_space=pltpu.HBM)
ANY = pl.BlockSpec(memory_space=pl.ANY)
SMEM = pl.BlockSpec(memory_space=pltpu.SMEM)
CHUNK = 256
F32 = jnp.float32
BF16 = jnp.bfloat16


def shape(*dims, dtype=F32):
    return jax.ShapeDtypeStruct(dims, dtype)


def params(mib):
    return pltpu.CompilerParams(vmem_limit_bytes=mib * MIB)


def cost(flops, mib):
    return pl.CostEstimate(flops=flops, bytes_accessed=int(mib * MIB), transcendentals=0)


def terms(value, count):
    parts = []
    for _ in range(count):
        part = value.astype(BF16)
        parts.append(part)
        value = value - part.astype(F32)
    return parts


def split(value, count):
    return jnp.concatenate(terms(value, count), 0)


def folded(value, count):
    rows = value.shape[0] // count
    total = value[:rows]
    for n in range(1, count):
        total = total + value[n * rows : (n + 1) * rows]
    return total


def dot(a, b, contract):
    return lax.dot_general(a, b, ((contract[:1], contract[1:]), ((), ())), preferred_element_type=F32)


def members(scalars_ref, flow):
    core = scalars_ref[0]
    return 2 * (1 - core) + flow, 2 * core + flow


def load_kernel(flow, scalars_ref, x_hbm, c_hbm, e_hbm, q_hbm, after_ref, x_ref, c_ref, e_ref, other_ref, own_ref, q_ref, sems):
    copies = []
    for slot, m in enumerate(members(scalars_ref, flow)):
        parts = [
            (q_hbm.at[m], q_ref.at[slot]),
            (c_hbm.at[m], c_ref.at[slot]),
            (x_hbm.at[m], x_ref.at[slot]),
        ] + [(e_hbm.at[0, m, pl.ds(n, 256)], e_ref.at[slot, pl.ds(n, 256)]) for n in range(0, 1024, 256)]
        started = []
        for n, (source, target) in enumerate(parts):
            copy = pltpu.make_async_copy(source, target, sems.at[slot, n])
            copy.start()
            started.append(copy)
        copies.append(started)
    for slot, out_ref in enumerate((other_ref, own_ref)):
        copies[slot][0].wait()
        q = split(q_ref[slot], 3)
        copies[slot][1].wait()
        y = split(folded(dot(q, c_ref[slot], (1, 1)), 3), 3)
        copies[slot][2].wait()
        out_ref[...] = folded(dot(y, x_ref[slot], (1, 0)), 3)
        for n in range(4):
            copies[slot][3 + n].wait()
            rows = pl.ds(256 * n, 256)
            out_ref[:, rows] += folded(dot(q, e_ref[slot, rows], (1, 1)), 3)


def load(flow, scalars, arrays, after):
    return pl.pallas_call(
        lambda *refs: load_kernel(flow, *refs),
        out_shape=[
            pltpu.VMEM((2, 512, 1024), BF16),
            pltpu.VMEM((2, 512, 1024), BF16),
            pltpu.VMEM((2, 1024, 1024), BF16),
            shape(32, 1024),
            shape(32, 1024),
        ],
        in_specs=[SMEM, HBM, HBM, HBM, HBM, ANY],
        out_specs=[VMEM] * 5,
        scratch_shapes=[pltpu.VMEM((2, 32, 1024), F32), pltpu.SemaphoreType.DMA((2, 7))],
        compiler_params=params(6),
        cost_estimate=cost(2 * 2 * 96 * 1024 * 2048, 9),
    )(scalars, *arrays, after)


def project_kernel(slot, x_ref, c_ref, e_ref, p_ref, after_ref, z_ref):
    p = split(p_ref[...], 3)
    w = split(folded(dot(p, x_ref[slot], (1, 1)), 3), 3)
    z_ref[...] = folded(dot(w, c_ref[slot], (1, 0)) + dot(p, e_ref[slot], (1, 0)), 3)


def project(slot, held, p, after):
    return pl.pallas_call(
        lambda *refs: project_kernel(slot, *refs),
        out_shape=shape(32, 1024),
        in_specs=[VMEM] * 4 + [ANY],
        out_specs=VMEM,
        compiler_params=params(6),
        cost_estimate=cost(2 * 96 * 1024 * 2048, 4),
    )(*held, p, after)


def gram_schmidt_kernel(p_ref, after_ref, basis_ref, factor_ref):
    value = p_ref[...]
    rows = lax.broadcasted_iota(jnp.int32, (32, 128), 0)
    lanes = lax.broadcasted_iota(jnp.int32, (32, 128), 1)
    factor = jnp.where(rows == lanes, 1.0, 0.0)
    for k in range(32):
        group = k // 8 * 8
        if k % 8 == 0 and k > 0:
            value, factor = value[8:], factor[8:]
        at = k - group
        row, factor_row = value[at : at + 1], factor[at : at + 1]
        dots = jnp.sum(value * row, axis=1, keepdims=True)
        square = dots[at : at + 1] + 1e-6
        scale = 1.0 / jnp.sqrt(square)
        basis_ref[k : k + 1, :] = row * scale
        factor_ref[k : k + 1, :] = factor_row * scale
        weights = dots * (1.0 / square)
        value = value - weights * row
        factor = factor - weights * factor_row


def gram_schmidt(p, after):
    return pl.pallas_call(
        gram_schmidt_kernel,
        out_shape=[shape(32, 1024), shape(32, 128)],
        in_specs=[VMEM, ANY],
        out_specs=[VMEM, VMEM],
        compiler_params=params(4),
        cost_estimate=cost(4_000_000, 8),
    )(p, after)


def flip_kernel(scalars_ref, other_ref, own_ref, other_left, own_left, other_rows, own_rows, flipped):
    start = pl.multiple_of(scalars_ref[1] * 8, 8)
    for basis_ref, left_ref, rows_ref in ((other_ref, other_left, other_rows), (own_ref, own_left, own_rows)):
        flipped[...] = basis_ref[...].T
        high, low = terms(flipped[...], 2)
        left_ref[...] = jnp.concatenate([high, high, low], 1)
        high, low = terms(flipped[pl.ds(start, 8), :], 2)
        rows_ref[...] = jnp.concatenate([high, high, low], 1).astype(F32)


def flip(scalars, other_basis, own_basis):
    return pl.pallas_call(
        flip_kernel,
        out_shape=[shape(1024, 96, dtype=BF16)] * 2 + [shape(8, 96)] * 2,
        in_specs=[SMEM, VMEM, VMEM],
        out_specs=[VMEM] * 4,
        scratch_shapes=[pltpu.VMEM((1024, 32), F32)],
        compiler_params=params(4),
        cost_estimate=cost(1_000_000, 3),
    )(scalars, other_basis, own_basis)


def merge_kernel(slot, x_ref, c_ref, e_ref, after_ref, merged_ref):
    for start in range(0, 1024, CHUNK):
        rows = pl.ds(start, CHUNK)
        product = dot(x_ref[slot, :, rows], c_ref[slot], (0, 0))
        merged_ref[rows] = product + e_ref[slot, rows].astype(F32)


def merge(slot, held, after):
    return pl.pallas_call(
        lambda *refs: merge_kernel(slot, *refs),
        out_shape=pltpu.VMEM((1024, 1024), F32),
        in_specs=[VMEM] * 3 + [ANY],
        out_specs=VMEM,
        compiler_params=params(6),
        cost_estimate=cost(2 * 512 * 1024 * 1024, 4),
    )(*held, after)


def solve_kernel(a_ref, b_ref, factor_ref, q_ref):
    f = terms(factor_ref[:, :32], 3)
    z = terms(a_ref[...] + b_ref[...], 3)
    pairs = ((0, 0), (0, 1), (0, 2), (1, 0), (1, 1), (2, 0))
    left = jnp.concatenate([f[i] for i, _ in pairs], 1)
    right = jnp.concatenate([z[j] for _, j in pairs], 0)
    q_ref[...] = dot(left, right, (1, 0)) * (1.0 / 128.0)


def solve(a, b, factor):
    return pl.pallas_call(
        solve_kernel,
        out_shape=shape(32, 1024),
        in_specs=[VMEM] * 3,
        out_specs=VMEM,
        compiler_params=params(4),
        cost_estimate=cost(2 * 32 * 192 * 1024, 1),
    )(a, b, factor)


def finish_flow(flow, scalars_ref, merged, lefts, qs, rows, outs, error_hbm, stage, sems):
    copies = []
    for slot, m in enumerate(members(scalars_ref, flow)):
        high, low = terms(qs[slot][...], 2)
        right = jnp.concatenate([high, low, high], 0)
        for n, start in enumerate(range(0, 1024, CHUNK)):
            block = pl.ds(start, CHUNK)
            product = dot(lefts[slot][block], right, (1, 0))
            stage[slot, block] = (merged[slot][block] - product).astype(BF16)
            copy = pltpu.make_async_copy(stage.at[slot, block], error_hbm.at[0, m, block], sems.at[slot, n])
            copy.start()
            copies.append(copy)
        outs[slot][...] = dot(rows[slot][...].astype(BF16), right, (1, 0))
    return copies


def finish_first_kernel(scalars_ref, *refs):
    merged, lefts, qs, rows = (refs[2 * n : 2 * n + 2] for n in range(4))
    error_hbm, other_out, own_out, stage, sems = refs[8:]
    for copy in finish_flow(0, scalars_ref, merged, lefts, qs, rows, (other_out, own_out), error_hbm, stage, sems):
        copy.wait()


def finish_first(scalars, merged, lefts, qs, rows):
    return pl.pallas_call(
        finish_first_kernel,
        out_shape=[shape(1, 4, 1024, 1024, dtype=BF16)] + [shape(8, 1024)] * 2,
        in_specs=[SMEM] + [VMEM] * 8,
        out_specs=[HBM, VMEM, VMEM],
        scratch_shapes=[pltpu.VMEM((2, 1024, 1024), BF16), pltpu.SemaphoreType.DMA((2, 1024 // CHUNK))],
        compiler_params=params(10),
        cost_estimate=cost(2 * 2 * 256 * 1024 * 1024, 4),
    )(scalars, *merged, *lefts, *qs, *rows)


def finish_last_kernel(scalars_ref, earlier_ref, *refs):
    merged, lefts, qs, rows, first_qs, first_outs = (refs[2 * n : 2 * n + 2] for n in range(6))
    error_hbm, update_hbm, new_q_hbm, outs, update, stage, sems, q_sems, update_sem = refs[12:]
    copies = []
    places = (*members(scalars_ref, 0), *members(scalars_ref, 1))
    for n, (m, q_ref) in enumerate(zip(places, (*first_qs, *qs))):
        copies.append(pltpu.make_async_copy(q_ref, new_q_hbm.at[m], q_sems.at[n]))
    for copy in copies:
        copy.start()
    flow_outs = (outs.at[0], outs.at[1])
    copies += finish_flow(1, scalars_ref, merged, lefts, qs, rows, flow_outs, error_hbm, stage, sems)
    for m, out_ref in zip(places, (*first_outs, *flow_outs)):
        update[m] = out_ref[...].astype(BF16)
    copies.append(pltpu.make_async_copy(update, update_hbm, update_sem))
    copies[-1].start()
    for copy in copies:
        copy.wait()


def finish_last(scalars, error, merged, lefts, qs, rows, first_qs, first_outs):
    return pl.pallas_call(
        finish_last_kernel,
        out_shape=[shape(1, 4, 1024, 1024, dtype=BF16), shape(4, 8, 1024, dtype=BF16), shape(4, 32, 1024)],
        in_specs=[SMEM, HBM] + [VMEM] * 12,
        out_specs=[HBM, HBM, HBM],
        scratch_shapes=[
            pltpu.VMEM((2, 8, 1024), F32),
            pltpu.VMEM((4, 8, 1024), BF16),
            pltpu.VMEM((2, 1024, 1024), BF16),
            pltpu.SemaphoreType.DMA((2, 1024 // CHUNK)),
            pltpu.SemaphoreType.DMA((4,)),
            pltpu.SemaphoreType.DMA,
        ],
        input_output_aliases={1: 0},
        compiler_params=params(10),
        cost_estimate=cost(2 * 2 * 256 * 1024 * 1024, 4),
    )(scalars, error, *merged, *lefts, *qs, *rows, *first_qs, *first_outs)


def other_core(value):
    return lax.ppermute(value, AXES, core_pairs())


def exchange(step, values):
    return [lax.ppermute(values[f], AXES, step_pairs(f, step)) for f in range(2)]


def added(values, received):
    return [a + b for a, b in zip(values, received)]


def on_device(inputs, cotangents, error_buffer, previous_q):
    scalars = jnp.stack([lax.axis_index("row") % 2, lax.axis_index(AXES)]).astype(jnp.int32)
    arrays = [pltpu.with_memory_space_constraint(a, pltpu.HBM) for a in (inputs, cotangents, error_buffer, previous_q)]
    held, sums, merged = [], [], [[None, None], [None, None]]
    after = jnp.zeros((8, 128), F32)
    for flow in range(2):
        *arrays_here, other, own = load(flow, scalars, arrays, after)
        held.append(arrays_here)
        after = own + other_core(other)
        sums.append(after)
    for step in range(6):
        received = exchange(step, sums)
        if step in (1, 2):
            merged[0][step - 1] = merge(step - 1, held[0], sums[1])
        sums = added(sums, received)
    means = [value * (1.0 / 128.0) for value in sums]
    other_means = [other_core(value) for value in means]
    sums, after = [], means[0]
    for flow in range(2):
        own = project(1, held[flow], means[flow], after)
        after = project(0, held[flow], other_means[flow], own)
        sums.append(own + other_core(after))
    bases, factors, lefts, rows = [], [], [], []
    for step in range(6):
        received = exchange(step, sums)
        if step < 2:
            basis, factor = gram_schmidt(means[step], sums[1])
            bases.append(basis)
            factors.append(factor)
        elif step < 4:
            merged[1][step - 2] = merge(step - 2, held[1], sums[1])
        if 1 <= step < 3:
            other_left, own_left, other_rows, own_rows = flip(scalars, other_core(bases[step - 1]), bases[step - 1])
            lefts.append((other_left, own_left))
            rows.append((other_rows, own_rows))
        if step < 5:
            sums = added(sums, received)
    own_qs = [solve(sums[f], received[f], factors[f]) for f in range(2)]
    qs = [(other_core(q), q) for q in own_qs]
    error, *outs = finish_first(scalars, merged[0], lefts[0], qs[0], rows[0])
    return finish_last(scalars, error, merged[1], lefts[1], qs[1], rows[1], qs[0], outs)


def solution(mesh):
    return jax.shard_map(
        on_device,
        mesh=mesh,
        in_specs=(
            P(None, AXES, None),
            P(None, AXES, None),
            P(AXES, None, None, None),
            P(),
        ),
        out_specs=(P(AXES, None, None, None), P(None, AXES, None), P()),
        check_vma=False,
    )
```

time: 464 us -> 111 us (0.24); the launches traced: 456 us -> 111 us
  waiting for transfers between devices: 292 us -> 19.7 us
  other arithmetic: 83.1 us -> 0.49 us
  matrix products: 62.2 us -> 0 us
  starting transfers between devices: 0.3 us -> 52.1 us
  Pallas kernels: 0 us -> 37.8 us
  between operations: 14.9 us -> 1.19 us
    psum x2 -> x0, waiting for transfers between devices: 292 us -> none  [the longest x1 148 us: on_device(): summed = lax.psum(local_p, ('row', 'col')) / devices]
    dot_general x4 -> x0, matrix products: 62.2 us -> none  [the longest x1 18.9 us: on_device(): local_p = jnp.einsum('mrj,mij->mri', previous_q, merged, precision=highest)]
    ppermute x0 -> x34, starting transfers between devices: none -> 52.1 us  [the longest x24 33.8 us: exchange(): lax.ppermute(values[f], AXES, step_pairs(f, step))]
    pallas_call x0 -> x18, Pallas kernels: none -> 37.8 us  [the longest x2 13.5 us: load(): pl.pallas_call(lambda *refs: load_kernel(flow, *refs), out_shape=[pltpu.V...]
    unnamed x25 -> x0, other arithmetic: 37.4 us -> none
    reduce_sum x91 -> x0, other arithmetic: 26.7 us -> none  [the longest x74 23.4 us: gram_schmidt(): jnp.sum(earlier * vector, axis=-1, keepdims=True) * earlier]
    ppermute x0 -> x34, waiting for transfers between devices: none -> 19.7 us  [the longest x24 18.7 us: exchange(): lax.ppermute(values[f], AXES, step_pairs(f, step))]
    broadcast_in_dim x1 -> x0, other arithmetic: 9.91 us -> none  [on_device(): new_error = (merged - decompressed).astype(jnp.bfloat16)[None]]
  transfers between devices with their start and end apart: 2 -> 34, of which waited for: 2 -> 12; matrix products, arithmetic and copies ran while one was open for 0% -> 0% of each run, Pallas kernels for 0% -> 19%
where the time goes in v1:
time: 111 us
  starting transfers between devices  52.1 us (47%)
  Pallas kernels  37.8 us (34%)
  waiting for transfers between devices  19.7 us (18%)
  between operations  1.19 us (1%)
    ppermute x24, starting transfers between devices, exchange(): lax.ppermute(values[f], AXES, step_pairs(f, step))  33.8 us
    ppermute x24, waiting for transfers between devices, exchange(): lax.ppermute(values[f], AXES, step_pairs(f, step))  18.7 us
    ppermute x10, starting transfers between devices, other_core(): return lax.ppermute(value, AXES, core_pairs())  18.3 us
    pallas_call x2, Pallas kernels, load(): pl.pallas_call(lambda *refs: load_kernel(flow, *refs), out_shape=[pltpu.V...  13.5 us
    pallas_call x2, Pallas kernels, gram_schmidt(): pl.pallas_call(gram_schmidt_kernel, out_shape=[shape(32, 1024), shape(32,...  6.33 us
    pallas_call x4, Pallas kernels, merge(): pl.pallas_call(lambda *refs: merge_kernel(slot, *refs), out_shape=pltpu.V...  5.22 us
    pallas_call x4, Pallas kernels, project(): pl.pallas_call(lambda *refs: project_kernel(slot, *refs), out_shape=shape...  3.76 us
    pallas_call x1, Pallas kernels, finish_last(): pl.pallas_call(finish_last_kernel, out_shape=[shape(1, 4, 1024, 1024, dty...  3.12 us
  transfers between devices with their start and end apart: 34, of which 12 were waited for; matrix products, arithmetic and copies ran while one was open for 0% of the time, Pallas kernels for 19%

profile of v1, /device:TPU:1, one launch (start us, length us, event | category | flops | bytes accessed | tf_op | source)
XLA Modules:
  0.0 111.3 jit_solution(6770361872734225164)
XLA Ops:
  0.7 6.8 %shard_map.67 = (bf16[2,512,1024]{2,1,0:T(8,128)(2,1)S(1)}, bf16[2,512,1024]{2,1,0:T(8,128)(2,1)S(1)}, bf16[2,1024,1024]{2,1,0:T(8,128)(2,1)S(1)}, f32[32,1024]{1,0:T(8,128)S(1)}, f32[32,1024]{1,0:T(8,128)S(1)}) custom-call(s32[2]{0:T(128)S(1)} %pad_add_fusion.refs_0_.scalars_ref, bf16[4,512,1024]{2,1,0:T(8,128)(2,1)} %refs_1_.3, ...), custom_call_target="tpu_custom_call" | custom-call | flops 805306368 | bytes 9437184 | tf_op jit(solution)/shard_map/pallas_call | solution.py:142
  7.5 1.5 %collective-permute-start = (f32[32,1024]{1,0:T(8,128)S(1)}, f32[32,1024]{1,0:T(8,128)S(1)}, u32[]{:S(2)}, u32[]{:S(2)}) collective-permute-start(f32[32,1024]{1,0:T(8,128)S(1)} %get-tuple-element.32), channel_id=1, source_target_pairs={{0,8},{1,9},{2,10},{3,11},{4,12},{5,13},{6,14},{7,15},{8,0},{9,1},... | collective-permute-start | bytes 393224 | tf_op jit(solution)/shard_map/ppermute | solution.py:343
  10.0 6.8 %shard_map.68 = (bf16[2,512,1024]{2,1,0:T(8,128)(2,1)S(1)}, bf16[2,512,1024]{2,1,0:T(8,128)(2,1)S(1)}, bf16[2,1024,1024]{2,1,0:T(8,128)(2,1)S(1)}, f32[32,1024]{1,0:T(8,128)S(1)}, f32[32,1024]{1,0:T(8,128)S(1)}) custom-call(s32[2]{0:T(128)S(1)} %pad_add_fusion.refs_0_.scalars_ref, bf16[4,512,1024]{2,1,0:T(8,128)(2,1)} %refs_1_.3, ...), custom_call_target="tpu_custom_call" | custom-call | flops 805306368 | bytes 9437184 | tf_op jit(solution)/shard_map/pallas_call | solution.py:142
  17.2 2.6 %collective-permute-start.4 = (f32[32,1024]{1,0:T(8,128)S(1)}, f32[32,1024]{1,0:T(8,128)S(1)}, u32[]{:S(2)}, u32[]{:S(2)}) collective-permute-start(f32[32,1024]{1,0:T(8,128)S(1)} %add.87.refs_5_), channel_id=1, source_target_pairs={{0,2},{1,3},{2,0},{3,1},{4,6},{5,7},{6,4},{7,5},{8,14},{9,15},{10,... | collective-permute-start | bytes 393224 | tf_op jit(solution)/shard_map/ppermute | solution.py:347
  19.8 2.8 %collective-permute-start.2 = (f32[32,1024]{1,0:T(8,128)S(1)}, f32[32,1024]{1,0:T(8,128)S(1)}, u32[]{:S(2)}, u32[]{:S(2)}) collective-permute-start(f32[32,1024]{1,0:T(8,128)S(1)} %add.88), channel_id=1, source_target_pairs={{0,16},{1,17},{2,18},{3,19},{4,20},{5,21},{6,22},{7,23},{8,56},{9,... | collective-permute-start | bytes 393224 | tf_op jit(solution)/shard_map/ppermute | solution.py:347
  22.6 2.5 %collective-permute-start.5 = (f32[32,1024]{1,0:T(8,128)S(1)}, f32[32,1024]{1,0:T(8,128)S(1)}, u32[]{:S(2)}, u32[]{:S(2)}) collective-permute-start(f32[32,1024]{1,0:T(8,128)S(1)} %add.91), channel_id=1, source_target_pairs={{0,16},{1,17},{2,18},{3,19},{4,20},{5,21},{6,22},{7,23},{8,56},{9,... | collective-permute-start | bytes 393224 | tf_op jit(solution)/shard_map/ppermute | solution.py:347
  25.2 3.8 %collective-permute-start.3 = (f32[32,1024]{1,0:T(8,128)S(1)}, f32[32,1024]{1,0:T(8,128)S(1)}, u32[]{:S(2)}, u32[]{:S(2)}) collective-permute-start(f32[32,1024]{1,0:T(8,128)S(1)} %add.89.refs_3_), channel_id=1, source_target_pairs={{0,1},{1,0},{2,3},{3,2},{4,5},{5,4},{6,7},{7,6},{8,73},{9,72},{10,... | collective-permute-start | bytes 393224 | tf_op jit(solution)/shard_map/ppermute | solution.py:347
  29.1 2.6 %collective-permute-start.6 = (f32[32,1024]{1,0:T(8,128)S(1)}, f32[32,1024]{1,0:T(8,128)S(1)}, u32[]{:S(2)}, u32[]{:S(2)}) collective-permute-start(f32[32,1024]{1,0:T(8,128)S(1)} %add.92), channel_id=1, source_target_pairs={{0,1},{1,0},{2,3},{3,2},{4,5},{5,4},{6,7},{7,6},{8,73},{9,72},{10,... | collective-permute-start | bytes 393224 | tf_op jit(solution)/shard_map/ppermute | solution.py:347
  31.8 2.7 %collective-permute-done.6 = f32[32,1024]{1,0:T(8,128)S(1)} collective-permute-done((f32[32,1024]{1,0:T(8,128)S(1)}, f32[32,1024]{1,0:T(8,128)S(1)}, u32[]{:S(2)}, u32[]{:S(2)}) %collective-permute-start.6) | collective-permute-done | bytes 131104 | tf_op jit(solution)/shard_map/ppermute | solution.py:347
  36.0 2.4 %collective-permute-done.7 = f32[32,1024]{1,0:T(8,128)S(1)} collective-permute-done((f32[32,1024]{1,0:T(8,128)S(1)}, f32[32,1024]{1,0:T(8,128)S(1)}, u32[]{:S(2)}, u32[]{:S(2)}) %collective-permute-start.7) | collective-permute-done | bytes 131104 | tf_op jit(solution)/shard_map/ppermute | solution.py:347
  39.7 2.6 %collective-permute-done.8 = f32[32,1024]{1,0:T(8,128)S(1)} collective-permute-done((f32[32,1024]{1,0:T(8,128)S(1)}, f32[32,1024]{1,0:T(8,128)S(1)}, u32[]{:S(2)}, u32[]{:S(2)}) %collective-permute-start.8) | collective-permute-done | bytes 131104 | tf_op jit(solution)/shard_map/ppermute | solution.py:347
  42.4 1.2 %collective-permute-done.12 = f32[32,1024]{1,0:T(8,128)S(1)} collective-permute-done((f32[32,1024]{1,0:T(8,128)S(1)}, f32[32,1024]{1,0:T(8,128)S(1)}, u32[]{:S(2)}, u32[]{:S(2)}) %collective-permute-start.12) | collective-permute-done | bytes 131104 | tf_op jit(solution)/shard_map/ppermute | solution.py:347
  43.7 2.4 %collective-permute-start.13 = (f32[32,1024]{1,0:T(8,128)S(1)}, f32[32,1024]{1,0:T(8,128)S(1)}, u32[]{:S(2)}, u32[]{:S(2)}) collective-permute-start(f32[32,1024]{1,0:T(8,128)S(1)} %add.99), channel_id=1, source_target_pairs={{0,2},{1,3},{2,0},{3,1},{4,6},{5,7},{6,4},{7,5},{8,14},{9,15},{10,... | collective-permute-start | bytes 393224 | tf_op jit(solution)/shard_map/ppermute | solution.py:347
  46.2 6.2 %collective-permute-start.14 = (f32[32,1024]{1,0:T(8,128)S(1)}, f32[32,1024]{1,0:T(8,128)S(1)}, u32[]{:S(2)}, u32[]{:S(2)}) collective-permute-start(f32[32,1024]{1,0:T(8,128)S(1)} %add_multiply_fusion.1.refs_3_.refs_4_.p_ref), channel_id=1, source_target_pairs={{0,8},{1,9},{2,10},{3,11},{4,12},{5,13},{6,14},{7,15},{8,0},{9,1},... | collective-permute-start | bytes 393224 | tf_op jit(solution)/shard_map/ppermute | solution.py:343
  52.5 1.9 %collective-permute-start.15 = (f32[32,1024]{1,0:T(8,128)S(1)}, f32[32,1024]{1,0:T(8,128)S(1)}, u32[]{:S(2)}, u32[]{:S(2)}) collective-permute-start(f32[32,1024]{1,0:T(8,128)S(1)} %add_multiply_fusion.refs_3_.p_ref), channel_id=1, source_target_pairs={{0,8},{1,9},{2,10},{3,11},{4,12},{5,13},{6,14},{7,15},{8,0},{9,1},... | collective-permute-start | bytes 393224 | tf_op jit(solution)/shard_map/ppermute | solution.py:343
  58.8 2.6 %collective-permute-start.19 = (f32[32,1024]{1,0:T(8,128)S(1)}, f32[32,1024]{1,0:T(8,128)S(1)}, u32[]{:S(2)}, u32[]{:S(2)}) collective-permute-start(f32[32,1024]{1,0:T(8,128)S(1)} %add.102), channel_id=1, source_target_pairs={{0,2},{1,3},{2,0},{3,1},{4,6},{5,7},{6,4},{7,5},{8,14},{9,15},{10,... | collective-permute-start | bytes 393224 | tf_op jit(solution)/shard_map/ppermute | solution.py:347
  61.4 3.0 %collective-permute-start.26 = (f32[32,1024]{1,0:T(8,128)S(1)}, f32[32,1024]{1,0:T(8,128)S(1)}, u32[]{:S(2)}, u32[]{:S(2)}) collective-permute-start(f32[32,1024]{1,0:T(8,128)S(1)} %add.101.after_ref), channel_id=1, source_target_pairs={{0,16},{1,17},{2,18},{3,19},{4,20},{5,21},{6,22},{7,23},{8,56},{9,... | collective-permute-start | bytes 393224 | tf_op jit(solution)/shard_map/ppermute | solution.py:347
  64.4 2.4 %collective-permute-start.20 = (f32[32,1024]{1,0:T(8,128)S(1)}, f32[32,1024]{1,0:T(8,128)S(1)}, u32[]{:S(2)}, u32[]{:S(2)}) collective-permute-start(f32[32,1024]{1,0:T(8,128)S(1)} %add.103), channel_id=1, source_target_pairs={{0,16},{1,17},{2,18},{3,19},{4,20},{5,21},{6,22},{7,23},{8,56},{9,... | collective-permute-start | bytes 393224 | tf_op jit(solution)/shard_map/ppermute | solution.py:347
  66.8 2.7 %collective-permute-start.27 = (f32[32,1024]{1,0:T(8,128)S(1)}, f32[32,1024]{1,0:T(8,128)S(1)}, u32[]{:S(2)}, u32[]{:S(2)}) collective-permute-start(f32[32,1024]{1,0:T(8,128)S(1)} %add.108.after_ref), channel_id=1, source_target_pairs={{0,1},{1,0},{2,3},{3,2},{4,5},{5,4},{6,7},{7,6},{8,73},{9,72},{10,... | collective-permute-start | bytes 393224 | tf_op jit(solution)/shard_map/ppermute | solution.py:347
  69.5 2.4 %collective-permute-start.21 = (f32[32,1024]{1,0:T(8,128)S(1)}, f32[32,1024]{1,0:T(8,128)S(1)}, u32[]{:S(2)}, u32[]{:S(2)}) collective-permute-start(f32[32,1024]{1,0:T(8,128)S(1)} %add.104), channel_id=1, source_target_pairs={{0,1},{1,0},{2,3},{3,2},{4,5},{5,4},{6,7},{7,6},{8,73},{9,72},{10,... | collective-permute-start | bytes 393224 | tf_op jit(solution)/shard_map/ppermute | solution.py:347
  72.0 2.9 %collective-permute-done.21 = f32[32,1024]{1,0:T(8,128)S(1)} collective-permute-done((f32[32,1024]{1,0:T(8,128)S(1)}, f32[32,1024]{1,0:T(8,128)S(1)}, u32[]{:S(2)}, u32[]{:S(2)}) %collective-permute-start.21) | collective-permute-done | bytes 131104 | tf_op jit(solution)/shard_map/ppermute | solution.py:347
  76.2 2.9 %collective-permute-done.22 = f32[32,1024]{1,0:T(8,128)S(1)} collective-permute-done((f32[32,1024]{1,0:T(8,128)S(1)}, f32[32,1024]{1,0:T(8,128)S(1)}, u32[]{:S(2)}, u32[]{:S(2)}) %collective-permute-start.22) | collective-permute-done | bytes 131104 | tf_op jit(solution)/shard_map/ppermute | solution.py:347
  80.1 3.2 %shard_map.75 = (f32[32,1024]{1,0:T(8,128)S(1)}, f32[32,128]{1,0:T(8,128)S(1)}) custom-call(f32[32,1024]{1,0:T(8,128)S(1)} %add_multiply_fusion.1.refs_3_.refs_4_.p_ref, f32[32,1024]{1,0:T(8,128)S(1)} %add.101.after_ref), custom_call_target="tpu_custom_call" | custom-call | flops 4000000 | bytes 8388608 | tf_op jit(solution)/shard_map/pallas_call | solution.py:198
  83.3 6.2 %collective-permute-start.17 = (f32[32,1024]{1,0:T(8,128)S(1)}, f32[32,1024]{1,0:T(8,128)S(1)}, u32[]{:S(2)}, u32[]{:S(2)}) collective-permute-start(f32[32,1024]{1,0:T(8,128)S(1)} %get-tuple-element.38.own_ref), channel_id=1, source_target_pairs={{0,8},{1,9},{2,10},{3,11},{4,12},{5,13},{6,14},{7,15},{8,0},{9,1},... | collective-permute-start | bytes 393224 | tf_op jit(solution)/shard_map/ppermute | solution.py:343
  89.6 1.3 %shard_map.69.refs_0_ = f32[1024,1024]{1,0:T(8,128)S(1)} custom-call(bf16[2,512,1024]{2,1,0:T(8,128)(2,1)S(1)} %get-tuple-element.28.refs_0_, bf16[2,512,1024]{2,1,0:T(8,128)(2,1)S(1)} %get-tuple-element.29.refs_1_, bf16[2,1024,1024]{2,1,0:T(8,128)(2,1)S(1)} %get-tuple-element.30.refs_2_, f32[32,1024]{1,0:T(8,128)S(1)} %add.89.refs_3_), custom_call_target="tpu_custom_call" | custom-call | flops 1073741824 | bytes 4194304 | tf_op jit(solution)/shard_map/pallas_call | solution.py:238
  90.9 3.2 %shard_map.81 = (f32[32,1024]{1,0:T(8,128)S(1)}, f32[32,128]{1,0:T(8,128)S(1)}) custom-call(f32[32,1024]{1,0:T(8,128)S(1)} %add_multiply_fusion.refs_3_.p_ref, f32[32,1024]{1,0:T(8,128)S(1)} %add.108.after_ref), custom_call_target="tpu_custom_call" | custom-call | flops 4000000 | bytes 8388608 | tf_op jit(solution)/shard_map/pallas_call | solution.py:198
  94.7 2.6 %collective-permute-start.32 = (f32[32,1024]{1,0:T(8,128)S(1)}, f32[32,1024]{1,0:T(8,128)S(1)}, u32[]{:S(2)}, u32[]{:S(2)}) collective-permute-start(f32[32,1024]{1,0:T(8,128)S(1)} %add.112.a_ref), channel_id=1, source_target_pairs={{0,2},{1,3},{2,0},{3,1},{4,6},{5,7},{6,4},{7,5},{8,14},{9,15},{10,... | collective-permute-start | bytes 393224 | tf_op jit(solution)/shard_map/ppermute | solution.py:347
  97.3 1.3 %shard_map.70.refs_1_ = f32[1024,1024]{1,0:T(8,128)S(1)} custom-call(bf16[2,512,1024]{2,1,0:T(8,128)(2,1)S(1)} %get-tuple-element.28.refs_0_, bf16[2,512,1024]{2,1,0:T(8,128)(2,1)S(1)} %get-tuple-element.29.refs_1_, bf16[2,1024,1024]{2,1,0:T(8,128)(2,1)S(1)} %get-tuple-element.30.refs_2_, f32[32,1024]{1,0:T(8,128)S(1)} %add.90.refs_3_), custom_call_target="tpu_custom_call" | custom-call | flops 1073741824 | bytes 4194304 | tf_op jit(solution)/shard_map/pallas_call | solution.py:238
  100.1 1.3 %shard_map.79.refs_0_ = f32[1024,1024]{1,0:T(8,128)S(1)} custom-call(bf16[2,512,1024]{2,1,0:T(8,128)(2,1)S(1)} %get-tuple-element.35.refs_0_, bf16[2,512,1024]{2,1,0:T(8,128)(2,1)S(1)} %get-tuple-element.36.refs_1_, bf16[2,1024,1024]{2,1,0:T(8,128)(2,1)S(1)} %get-tuple-element.37.refs_2_, f32[32,1024]{1,0:T(8,128)S(1)} %add.109.refs_3_), custom_call_target="tpu_custom_call" | custom-call | flops 1073741824 | bytes 4194304 | tf_op jit(solution)/shard_map/pallas_call | solution.py:238
  103.7 1.3 %shard_map.80.refs_1_ = f32[1024,1024]{1,0:T(8,128)S(1)} custom-call(bf16[2,512,1024]{2,1,0:T(8,128)(2,1)S(1)} %get-tuple-element.35.refs_0_, bf16[2,512,1024]{2,1,0:T(8,128)(2,1)S(1)} %get-tuple-element.36.refs_1_, bf16[2,1024,1024]{2,1,0:T(8,128)(2,1)S(1)} %get-tuple-element.37.refs_2_, f32[32,1024]{1,0:T(8,128)S(1)} %add.110.refs_3_), custom_call_target="tpu_custom_call" | custom-call | flops 1073741824 | bytes 4194304 | tf_op jit(solution)/shard_map/pallas_call | solution.py:238
  105.1 2.9 %shard_map.78 = (bf16[1,4,1024,1024]{3,2,1,0:T(8,128)(2,1)}, f32[8,1024]{1,0:T(8,128)S(1)}, f32[8,1024]{1,0:T(8,128)S(1)}) custom-call(s32[2]{0:T(128)S(1)} %pad_add_fusion.refs_0_.scalars_ref, f32[1024,1024]{1,0:T(8,128)S(1)} %shard_map.69.refs_0_, f32[1024,1024]{1,0:T(8,128)S(1)} %shard_map.70.refs_1_, bf16[1024,96]{1,0:T(8,128)(2,1)S(1)} %get-tuple-element.39.refs_2_, ...), custom_call_target="tpu_custom_call" | custom-call | flops 1073741824 | bytes 4194304 | tf_op jit(solution)/shard_map/pallas_call | solution.py:292
  108.0 3.1 %shard_map.84 = (bf16[1,4,1024,1024]{3,2,1,0:T(8,128)(2,1)}, bf16[4,8,1024]{2,1,0:T(8,128)(2,1)}, f32[4,32,1024]{2,1,0:T(8,128)}) custom-call(s32[2]{0:T(128)S(1)} %pad_add_fusion.refs_0_.scalars_ref, bf16[1,4,1024,1024]{3,2,1,0:T(8,128)(2,1)} %get-tuple-element.44.earlier_ref, f32[1024,1024]{1,0:T(8,128)S(1)} %shard_map.79.refs_0_, ...), custom_call_target="tpu_custom_call", output_to_operand_aliasing={{0}: (1, {})} | custom-call | flops 1073741824 | bytes 4194304 | tf_op jit(solution)/shard_map/pallas_call | solution.py:323
  (82 shorter events, 16.1 us)
Async XLA Ops:
  16.8 3.0 %collective-permute-start.1 = (f32[32,1024]{1,0:T(8,128)S(1)}, f32[32,1024]{1,0:T(8,128)S(1)}, u32[]{:S(2)}, u32[]{:S(2)}) collective-permute-start(f32[32,1024]{1,0:T(8,128)S(1)} %get-tuple-element.34), channel_id=1, source_target_pairs={{0,8},{1,9},{2,10},{3,11},{4,12},{5,13},{6,14},{7,15},{8,0},{9,1},... | collective-permute-start | bytes 393224 | tf_op jit(solution)/shard_map/ppermute | solution.py:343
  17.2 5.4 %collective-permute-start.4 = (f32[32,1024]{1,0:T(8,128)S(1)}, f32[32,1024]{1,0:T(8,128)S(1)}, u32[]{:S(2)}, u32[]{:S(2)}) collective-permute-start(f32[32,1024]{1,0:T(8,128)S(1)} %add.87.refs_5_), channel_id=1, source_target_pairs={{0,2},{1,3},{2,0},{3,1},{4,6},{5,7},{6,4},{7,5},{8,14},{9,15},{10,... | collective-permute-start | bytes 393224 | tf_op jit(solution)/shard_map/ppermute | solution.py:347
  19.8 5.4 %collective-permute-start.2 = (f32[32,1024]{1,0:T(8,128)S(1)}, f32[32,1024]{1,0:T(8,128)S(1)}, u32[]{:S(2)}, u32[]{:S(2)}) collective-permute-start(f32[32,1024]{1,0:T(8,128)S(1)} %add.88), channel_id=1, source_target_pairs={{0,16},{1,17},{2,18},{3,19},{4,20},{5,21},{6,22},{7,23},{8,56},{9,... | collective-permute-start | bytes 393224 | tf_op jit(solution)/shard_map/ppermute | solution.py:347
  22.6 6.4 %collective-permute-start.5 = (f32[32,1024]{1,0:T(8,128)S(1)}, f32[32,1024]{1,0:T(8,128)S(1)}, u32[]{:S(2)}, u32[]{:S(2)}) collective-permute-start(f32[32,1024]{1,0:T(8,128)S(1)} %add.91), channel_id=1, source_target_pairs={{0,16},{1,17},{2,18},{3,19},{4,20},{5,21},{6,22},{7,23},{8,56},{9,... | collective-permute-start | bytes 393224 | tf_op jit(solution)/shard_map/ppermute | solution.py:347
  25.2 6.4 %collective-permute-start.3 = (f32[32,1024]{1,0:T(8,128)S(1)}, f32[32,1024]{1,0:T(8,128)S(1)}, u32[]{:S(2)}, u32[]{:S(2)}) collective-permute-start(f32[32,1024]{1,0:T(8,128)S(1)} %add.89.refs_3_), channel_id=1, source_target_pairs={{0,1},{1,0},{2,3},{3,2},{4,5},{5,4},{6,7},{7,6},{8,73},{9,72},{10,... | collective-permute-start | bytes 393224 | tf_op jit(solution)/shard_map/ppermute | solution.py:347
  29.1 5.4 %collective-permute-start.6 = (f32[32,1024]{1,0:T(8,128)S(1)}, f32[32,1024]{1,0:T(8,128)S(1)}, u32[]{:S(2)}, u32[]{:S(2)}) collective-permute-start(f32[32,1024]{1,0:T(8,128)S(1)} %add.92), channel_id=1, source_target_pairs={{0,1},{1,0},{2,3},{3,2},{4,5},{5,4},{6,7},{7,6},{8,73},{9,72},{10,... | collective-permute-start | bytes 393224 | tf_op jit(solution)/shard_map/ppermute | solution.py:347
  31.6 3.9 %collective-permute-start.10 = (f32[32,1024]{1,0:T(8,128)S(1)}, f32[32,1024]{1,0:T(8,128)S(1)}, u32[]{:S(2)}, u32[]{:S(2)}) collective-permute-start(f32[32,1024]{1,0:T(8,128)S(1)} %add.90.refs_3_), channel_id=1, source_target_pairs={{0,6},{1,7},{2,4},{3,5},{4,2},{5,3},{6,0},{7,1},{8,10},{9,11},{10,... | collective-permute-start | bytes 393224 | tf_op jit(solution)/shard_map/ppermute | solution.py:347
  34.5 3.9 %collective-permute-start.7 = (f32[32,1024]{1,0:T(8,128)S(1)}, f32[32,1024]{1,0:T(8,128)S(1)}, u32[]{:S(2)}, u32[]{:S(2)}) collective-permute-start(f32[32,1024]{1,0:T(8,128)S(1)} %add.93), channel_id=1, source_target_pairs={{0,6},{1,7},{2,4},{3,5},{4,2},{5,3},{6,0},{7,1},{8,10},{9,11},{10,... | collective-permute-start | bytes 393224 | tf_op jit(solution)/shard_map/ppermute | solution.py:347
  35.5 3.9 %collective-permute-start.11 = (f32[32,1024]{1,0:T(8,128)S(1)}, f32[32,1024]{1,0:T(8,128)S(1)}, u32[]{:S(2)}, u32[]{:S(2)}) collective-permute-start(f32[32,1024]{1,0:T(8,128)S(1)} %add.97), channel_id=1, source_target_pairs={{0,48},{1,49},{2,50},{3,51},{4,52},{5,53},{6,54},{7,55},{8,24},{9,... | collective-permute-start | bytes 393224 | tf_op jit(solution)/shard_map/ppermute | solution.py:347
  38.4 3.9 %collective-permute-start.8 = (f32[32,1024]{1,0:T(8,128)S(1)}, f32[32,1024]{1,0:T(8,128)S(1)}, u32[]{:S(2)}, u32[]{:S(2)}) collective-permute-start(f32[32,1024]{1,0:T(8,128)S(1)} %add.94), channel_id=1, source_target_pairs={{0,48},{1,49},{2,50},{3,51},{4,52},{5,53},{6,54},{7,55},{8,24},{9,... | collective-permute-start | bytes 393224 | tf_op jit(solution)/shard_map/ppermute | solution.py:347
  39.5 4.2 %collective-permute-start.12 = (f32[32,1024]{1,0:T(8,128)S(1)}, f32[32,1024]{1,0:T(8,128)S(1)}, u32[]{:S(2)}, u32[]{:S(2)}) collective-permute-start(f32[32,1024]{1,0:T(8,128)S(1)} %add.98), channel_id=1, source_target_pairs={{0,65},{1,64},{2,67},{3,66},{4,69},{5,68},{6,71},{7,70},{8,9},{9,8... | collective-permute-start | bytes 393224 | tf_op jit(solution)/shard_map/ppermute | solution.py:347
  42.3 3.9 %collective-permute-start.9 = (f32[32,1024]{1,0:T(8,128)S(1)}, f32[32,1024]{1,0:T(8,128)S(1)}, u32[]{:S(2)}, u32[]{:S(2)}) collective-permute-start(f32[32,1024]{1,0:T(8,128)S(1)} %add.95), channel_id=1, source_target_pairs={{0,65},{1,64},{2,67},{3,66},{4,69},{5,68},{6,71},{7,70},{8,9},{9,8... | collective-permute-start | bytes 393224 | tf_op jit(solution)/shard_map/ppermute | solution.py:347
  43.7 8.8 %collective-permute-start.13 = (f32[32,1024]{1,0:T(8,128)S(1)}, f32[32,1024]{1,0:T(8,128)S(1)}, u32[]{:S(2)}, u32[]{:S(2)}) collective-permute-start(f32[32,1024]{1,0:T(8,128)S(1)} %add.99), channel_id=1, source_target_pairs={{0,2},{1,3},{2,0},{3,1},{4,6},{5,7},{6,4},{7,5},{8,14},{9,15},{10,... | collective-permute-start | bytes 393224 | tf_op jit(solution)/shard_map/ppermute | solution.py:347
  46.2 9.1 %collective-permute-start.14 = (f32[32,1024]{1,0:T(8,128)S(1)}, f32[32,1024]{1,0:T(8,128)S(1)}, u32[]{:S(2)}, u32[]{:S(2)}) collective-permute-start(f32[32,1024]{1,0:T(8,128)S(1)} %add_multiply_fusion.1.refs_3_.refs_4_.p_ref), channel_id=1, source_target_pairs={{0,8},{1,9},{2,10},{3,11},{4,12},{5,13},{6,14},{7,15},{8,0},{9,1},... | collective-permute-start | bytes 393224 | tf_op jit(solution)/shard_map/ppermute | solution.py:343
  52.5 4.8 %collective-permute-start.15 = (f32[32,1024]{1,0:T(8,128)S(1)}, f32[32,1024]{1,0:T(8,128)S(1)}, u32[]{:S(2)}, u32[]{:S(2)}) collective-permute-start(f32[32,1024]{1,0:T(8,128)S(1)} %add_multiply_fusion.refs_3_.p_ref), channel_id=1, source_target_pairs={{0,8},{1,9},{2,10},{3,11},{4,12},{5,13},{6,14},{7,15},{8,0},{9,1},... | collective-permute-start | bytes 393224 | tf_op jit(solution)/shard_map/ppermute | solution.py:343
  58.3 3.1 %collective-permute-start.16 = (f32[32,1024]{1,0:T(8,128)S(1)}, f32[32,1024]{1,0:T(8,128)S(1)}, u32[]{:S(2)}, u32[]{:S(2)}) collective-permute-start(f32[32,1024]{1,0:T(8,128)S(1)} %shard_map.74), channel_id=1, source_target_pairs={{0,8},{1,9},{2,10},{3,11},{4,12},{5,13},{6,14},{7,15},{8,0},{9,1},... | collective-permute-start | bytes 393224 | tf_op jit(solution)/shard_map/ppermute | solution.py:343
  58.8 5.6 %collective-permute-start.19 = (f32[32,1024]{1,0:T(8,128)S(1)}, f32[32,1024]{1,0:T(8,128)S(1)}, u32[]{:S(2)}, u32[]{:S(2)}) collective-permute-start(f32[32,1024]{1,0:T(8,128)S(1)} %add.102), channel_id=1, source_target_pairs={{0,2},{1,3},{2,0},{3,1},{4,6},{5,7},{6,4},{7,5},{8,14},{9,15},{10,... | collective-permute-start | bytes 393224 | tf_op jit(solution)/shard_map/ppermute | solution.py:347
  61.4 5.4 %collective-permute-start.26 = (f32[32,1024]{1,0:T(8,128)S(1)}, f32[32,1024]{1,0:T(8,128)S(1)}, u32[]{:S(2)}, u32[]{:S(2)}) collective-permute-start(f32[32,1024]{1,0:T(8,128)S(1)} %add.101.after_ref), channel_id=1, source_target_pairs={{0,16},{1,17},{2,18},{3,19},{4,20},{5,21},{6,22},{7,23},{8,56},{9,... | collective-permute-start | bytes 393224 | tf_op jit(solution)/shard_map/ppermute | solution.py:347
  64.4 5.1 %collective-permute-start.20 = (f32[32,1024]{1,0:T(8,128)S(1)}, f32[32,1024]{1,0:T(8,128)S(1)}, u32[]{:S(2)}, u32[]{:S(2)}) collective-permute-start(f32[32,1024]{1,0:T(8,128)S(1)} %add.103), channel_id=1, source_target_pairs={{0,16},{1,17},{2,18},{3,19},{4,20},{5,21},{6,22},{7,23},{8,56},{9,... | collective-permute-start | bytes 393224 | tf_op jit(solution)/shard_map/ppermute | solution.py:347
  66.8 5.1 %collective-permute-start.27 = (f32[32,1024]{1,0:T(8,128)S(1)}, f32[32,1024]{1,0:T(8,128)S(1)}, u32[]{:S(2)}, u32[]{:S(2)}) collective-permute-start(f32[32,1024]{1,0:T(8,128)S(1)} %add.108.after_ref), channel_id=1, source_target_pairs={{0,1},{1,0},{2,3},{3,2},{4,5},{5,4},{6,7},{7,6},{8,73},{9,72},{10,... | collective-permute-start | bytes 393224 | tf_op jit(solution)/shard_map/ppermute | solution.py:347
  69.5 5.4 %collective-permute-start.21 = (f32[32,1024]{1,0:T(8,128)S(1)}, f32[32,1024]{1,0:T(8,128)S(1)}, u32[]{:S(2)}, u32[]{:S(2)}) collective-permute-start(f32[32,1024]{1,0:T(8,128)S(1)} %add.104), channel_id=1, source_target_pairs={{0,1},{1,0},{2,3},{3,2},{4,5},{5,4},{6,7},{7,6},{8,73},{9,72},{10,... | collective-permute-start | bytes 393224 | tf_op jit(solution)/shard_map/ppermute | solution.py:347
  71.9 4.2 %collective-permute-start.28 = (f32[32,1024]{1,0:T(8,128)S(1)}, f32[32,1024]{1,0:T(8,128)S(1)}, u32[]{:S(2)}, u32[]{:S(2)}) collective-permute-start(f32[32,1024]{1,0:T(8,128)S(1)} %add.109.refs_3_), channel_id=1, source_target_pairs={{0,6},{1,7},{2,4},{3,5},{4,2},{5,3},{6,0},{7,1},{8,10},{9,11},{10,... | collective-permute-start | bytes 393224 | tf_op jit(solution)/shard_map/ppermute | solution.py:347
  75.0 4.2 %collective-permute-start.22 = (f32[32,1024]{1,0:T(8,128)S(1)}, f32[32,1024]{1,0:T(8,128)S(1)}, u32[]{:S(2)}, u32[]{:S(2)}) collective-permute-start(f32[32,1024]{1,0:T(8,128)S(1)} %add.105), channel_id=1, source_target_pairs={{0,6},{1,7},{2,4},{3,5},{4,2},{5,3},{6,0},{7,1},{8,10},{9,11},{10,... | collective-permute-start | bytes 393224 | tf_op jit(solution)/shard_map/ppermute | solution.py:347
  76.1 3.9 %collective-permute-start.30 = (f32[32,1024]{1,0:T(8,128)S(1)}, f32[32,1024]{1,0:T(8,128)S(1)}, u32[]{:S(2)}, u32[]{:S(2)}) collective-permute-start(f32[32,1024]{1,0:T(8,128)S(1)} %add.110.refs_3_), channel_id=1, source_target_pairs={{0,48},{1,49},{2,50},{3,51},{4,52},{5,53},{6,54},{7,55},{8,24},{9,... | collective-permute-start | bytes 393224 | tf_op jit(solution)/shard_map/ppermute | solution.py:347
  79.2 10.4 %collective-permute-start.23 = (f32[32,1024]{1,0:T(8,128)S(1)}, f32[32,1024]{1,0:T(8,128)S(1)}, u32[]{:S(2)}, u32[]{:S(2)}) collective-permute-start(f32[32,1024]{1,0:T(8,128)S(1)} %add.106), channel_id=1, source_target_pairs={{0,48},{1,49},{2,50},{3,51},{4,52},{5,53},{6,54},{7,55},{8,24},{9,... | collective-permute-start | bytes 393224 | tf_op jit(solution)/shard_map/ppermute | solution.py:347
  80.0 14.6 %collective-permute-start.31 = (f32[32,1024]{1,0:T(8,128)S(1)}, f32[32,1024]{1,0:T(8,128)S(1)}, u32[]{:S(2)}, u32[]{:S(2)}) collective-permute-start(f32[32,1024]{1,0:T(8,128)S(1)} %add.111), channel_id=1, source_target_pairs={{0,65},{1,64},{2,67},{3,66},{4,69},{5,68},{6,71},{7,70},{8,9},{9,8... | collective-permute-start | bytes 393224 | tf_op jit(solution)/shard_map/ppermute | solution.py:347
  83.3 15.2 %collective-permute-start.17 = (f32[32,1024]{1,0:T(8,128)S(1)}, f32[32,1024]{1,0:T(8,128)S(1)}, u32[]{:S(2)}, u32[]{:S(2)}) collective-permute-start(f32[32,1024]{1,0:T(8,128)S(1)} %get-tuple-element.38.own_ref), channel_id=1, source_target_pairs={{0,8},{1,9},{2,10},{3,11},{4,12},{5,13},{6,14},{7,15},{8,0},{9,1},... | collective-permute-start | bytes 393224 | tf_op jit(solution)/shard_map/ppermute | solution.py:343
  89.6 10.3 %collective-permute-start.24 = (f32[32,1024]{1,0:T(8,128)S(1)}, f32[32,1024]{1,0:T(8,128)S(1)}, u32[]{:S(2)}, u32[]{:S(2)}) collective-permute-start(f32[32,1024]{1,0:T(8,128)S(1)} %add.107.a_ref), channel_id=1, source_target_pairs={{0,65},{1,64},{2,67},{3,66},{4,69},{5,68},{6,71},{7,70},{8,9},{9,8... | collective-permute-start | bytes 393224 | tf_op jit(solution)/shard_map/ppermute | solution.py:347
  94.1 7.3 %collective-permute-start.29 = (f32[32,1024]{1,0:T(8,128)S(1)}, f32[32,1024]{1,0:T(8,128)S(1)}, u32[]{:S(2)}, u32[]{:S(2)}) collective-permute-start(f32[32,1024]{1,0:T(8,128)S(1)} %get-tuple-element.45.own_ref), channel_id=1, source_target_pairs={{0,8},{1,9},{2,10},{3,11},{4,12},{5,13},{6,14},{7,15},{8,0},{9,1},... | collective-permute-start | bytes 393224 | tf_op jit(solution)/shard_map/ppermute | solution.py:343
  94.7 8.0 %collective-permute-start.32 = (f32[32,1024]{1,0:T(8,128)S(1)}, f32[32,1024]{1,0:T(8,128)S(1)}, u32[]{:S(2)}, u32[]{:S(2)}) collective-permute-start(f32[32,1024]{1,0:T(8,128)S(1)} %add.112.a_ref), channel_id=1, source_target_pairs={{0,2},{1,3},{2,0},{3,1},{4,6},{5,7},{6,4},{7,5},{8,14},{9,15},{10,... | collective-permute-start | bytes 393224 | tf_op jit(solution)/shard_map/ppermute | solution.py:347
  100.0 5.0 %collective-permute-start.25 = (f32[32,1024]{1,0:T(8,128)S(1)}, f32[32,1024]{1,0:T(8,128)S(1)}, u32[]{:S(2)}, u32[]{:S(2)}) collective-permute-start(f32[32,1024]{1,0:T(8,128)S(1)} %shard_map.77.refs_5_.refs_9_), channel_id=1, source_target_pairs={{0,8},{1,9},{2,10},{3,11},{4,12},{5,13},{6,14},{7,15},{8,0},{9,1},... | collective-permute-start | bytes 393224 | tf_op jit(solution)/shard_map/ppermute | solution.py:343
  102.9 5.0 %collective-permute-start.33 = (f32[32,1024]{1,0:T(8,128)S(1)}, f32[32,1024]{1,0:T(8,128)S(1)}, u32[]{:S(2)}, u32[]{:S(2)}) collective-permute-start(f32[32,1024]{1,0:T(8,128)S(1)} %shard_map.83.refs_5_), channel_id=1, source_target_pairs={{0,8},{1,9},{2,10},{3,11},{4,12},{5,13},{6,14},{7,15},{8,0},{9,1},... | collective-permute-start | bytes 393224 | tf_op jit(solution)/shard_map/ppermute | solution.py:343
  (2 other events, 5.0 us)

commit v2 on v1

v2 whole, which is shorter than its diff:
```python
import jax
import jax.numpy as jnp
from jax import lax
from jax.experimental import pallas as pl
from jax.experimental.pallas import tpu as pltpu
from jax.sharding import PartitionSpec as P

AXES = ("row", "col")
SIZES = (("zh", 2), ("y", 4), ("core", 2), ("x", 4), ("zl", 2))
ORDERS = (("x", "y", "z"), ("y", "z", "x"))


def coords_of(index):
    coords = {}
    for name, size in reversed(SIZES):
        coords[name] = index % size
        index //= size
    return coords


def index_of(coords):
    index = 0
    for name, size in SIZES:
        index = index * size + coords[name]
    return index


def partner(index, axis, mask):
    coords = coords_of(index)
    if axis == "z":
        z = (2 * coords["zh"] + coords["zl"]) ^ mask
        coords["zh"], coords["zl"] = z // 2, z % 2
    else:
        coords[axis] ^= mask
    return index_of(coords)


def step_pairs(step, mask):
    return [(index, partner(index, ORDERS[coords_of(index)["core"]][step], mask)) for index in range(128)]


def core_pairs():
    pairs = []
    for index in range(128):
        coords = coords_of(index)
        coords["core"] ^= 1
        pairs.append((index, index_of(coords)))
    return pairs


def other_core(value):
    return lax.ppermute(value, AXES, core_pairs())


MIB = 1024 * 1024
VMEM = pl.BlockSpec(memory_space=pltpu.VMEM)
HBM = pl.BlockSpec(memory_space=pltpu.HBM)
ANY = pl.BlockSpec(memory_space=pl.ANY)
SMEM = pl.BlockSpec(memory_space=pltpu.SMEM)
CHUNK = 256
F32 = jnp.float32
BF16 = jnp.bfloat16


def shape(*dims, dtype=F32):
    return jax.ShapeDtypeStruct(dims, dtype)


def params(mib):
    return pltpu.CompilerParams(vmem_limit_bytes=mib * MIB)


def cost(flops, mib):
    return pl.CostEstimate(flops=flops, bytes_accessed=int(mib * MIB), transcendentals=0)


def terms(value, count):
    parts = []
    for _ in range(count):
        part = value.astype(BF16)
        parts.append(part)
        value = value - part.astype(F32)
    return parts


def split(value, count):
    return jnp.concatenate(terms(value, count), 0)


def folded(value, count):
    rows = value.shape[0] // count
    total = value[:rows]
    for n in range(1, count):
        total = total + value[n * rows : (n + 1) * rows]
    return total


def dot(a, b, contract):
    return lax.dot_general(a, b, ((contract[:1], contract[1:]), ((), ())), preferred_element_type=F32)


def members(scalars_ref, side):
    core = scalars_ref[0]
    first = 2 * core if side else 2 * (1 - core)
    return first, first + 1


def load_kernel(side, scalars_ref, x_hbm, c_hbm, e_hbm, q_hbm, x_ref, c_ref, e_ref, p_ref, q_ref, sems):
    copies = []
    for slot, m in enumerate(members(scalars_ref, side)):
        parts = [
            (q_hbm.at[m], q_ref.at[slot]),
            (c_hbm.at[m], c_ref.at[slot]),
            (x_hbm.at[m], x_ref.at[slot]),
        ] + [(e_hbm.at[0, m, pl.ds(n, 512)], e_ref.at[slot, pl.ds(n, 512)]) for n in range(0, 1024, 512)]
        started = []
        for n, (source, target) in enumerate(parts):
            copy = pltpu.make_async_copy(source, target, sems.at[slot, n])
            copy.start()
            started.append(copy)
        copies.append(started)
    for slot in range(2):
        copies[slot][0].wait()
        q = split(q_ref[slot], 3)
        copies[slot][1].wait()
        y = split(folded(dot(q, c_ref[slot], (1, 1)), 3), 3)
        copies[slot][2].wait()
        p_ref[slot] = folded(dot(y, x_ref[slot], (1, 0)), 3)
        for n in range(2):
            copies[slot][3 + n].wait()
            rows = pl.ds(512 * n, 512)
            p_ref[slot, :, rows] += folded(dot(q, e_ref[slot, rows], (1, 1)), 3)


def load(side, scalars, arrays):
    return pl.pallas_call(
        lambda *refs: load_kernel(side, *refs),
        out_shape=[
            pltpu.VMEM((2, 512, 1024), BF16),
            pltpu.VMEM((2, 512, 1024), BF16),
            pltpu.VMEM((2, 1024, 1024), BF16),
            shape(2, 32, 1024),
        ],
        in_specs=[SMEM, HBM, HBM, HBM, HBM],
        out_specs=[VMEM] * 4,
        scratch_shapes=[pltpu.VMEM((2, 32, 1024), F32), pltpu.SemaphoreType.DMA((2, 5))],
        compiler_params=params(6),
        cost_estimate=cost(2 * 2 * 96 * 1024 * 2048, 9),
    )(scalars, *arrays)


def project_kernel(x_ref, c_ref, e_ref, p_ref, after_ref, z_ref):
    for slot in range(2):
        p = split(p_ref[slot], 3)
        w = split(folded(dot(p, x_ref[slot], (1, 1)), 3), 3)
        z_ref[slot] = folded(dot(w, c_ref[slot], (1, 0)) + dot(p, e_ref[slot], (1, 0)), 3)


def project(held, p, after):
    return pl.pallas_call(
        project_kernel,
        out_shape=shape(2, 32, 1024),
        in_specs=[VMEM] * 4 + [ANY],
        out_specs=VMEM,
        compiler_params=params(6),
        cost_estimate=cost(2 * 2 * 96 * 1024 * 2048, 8),
    )(*held, p, after)


def gram_schmidt_kernel(slot, p_ref, after_ref, basis_ref, factor_ref):
    value = p_ref[slot]
    rows = lax.broadcasted_iota(jnp.int32, (32, 128), 0)
    lanes = lax.broadcasted_iota(jnp.int32, (32, 128), 1)
    factor = jnp.where(rows == lanes, 1.0, 0.0)
    for k in range(32):
        group = k // 8 * 8
        if k % 8 == 0 and k > 0:
            value, factor = value[8:], factor[8:]
        at = k - group
        row, factor_row = value[at : at + 1], factor[at : at + 1]
        dots = jnp.sum(value * row, axis=1, keepdims=True)
        square = dots[at : at + 1] + 1e-6
        scale = 1.0 / jnp.sqrt(square)
        basis_ref[k : k + 1, :] = row * scale
        factor_ref[k : k + 1, :] = factor_row * scale
        weights = dots * (1.0 / square)
        value = value - weights * row
        factor = factor - weights * factor_row


def gram_schmidt(slot, p, after):
    return pl.pallas_call(
        lambda *refs: gram_schmidt_kernel(slot, *refs),
        out_shape=[shape(32, 1024), shape(32, 128)],
        in_specs=[VMEM, ANY],
        out_specs=[VMEM, VMEM],
        compiler_params=params(4),
        cost_estimate=cost(4_000_000, 8),
    )(p, after)


def flip_kernel(scalars_ref, first_ref, second_ref, after_ref, first_left, second_left, first_rows, second_rows, flipped):
    start = pl.multiple_of(scalars_ref[1] * 8, 8)
    for basis_ref, left_ref, rows_ref in ((first_ref, first_left, first_rows), (second_ref, second_left, second_rows)):
        flipped[...] = basis_ref[...].T
        high, low = terms(flipped[...], 2)
        left_ref[...] = jnp.concatenate([high, high, low], 1)
        high, low = terms(flipped[pl.ds(start, 8), :], 2)
        rows_ref[...] = jnp.concatenate([high, high, low], 1).astype(F32)


def flip(scalars, bases, after):
    return pl.pallas_call(
        flip_kernel,
        out_shape=[shape(1024, 96, dtype=BF16)] * 2 + [shape(8, 96)] * 2,
        in_specs=[SMEM, VMEM, VMEM, ANY],
        out_specs=[VMEM] * 4,
        scratch_shapes=[pltpu.VMEM((1024, 32), F32)],
        compiler_params=params(4),
        cost_estimate=cost(1_000_000, 3),
    )(scalars, *bases, after)


def merge_kernel(slot, x_ref, c_ref, e_ref, after_ref, merged_ref):
    for start in range(0, 1024, CHUNK):
        rows = pl.ds(start, CHUNK)
        product = dot(x_ref[slot, :, rows], c_ref[slot], (0, 0))
        merged_ref[rows] = product + e_ref[slot, rows].astype(F32)


def merge(slot, held, after):
    return pl.pallas_call(
        lambda *refs: merge_kernel(slot, *refs),
        out_shape=pltpu.VMEM((1024, 1024), F32),
        in_specs=[VMEM] * 3 + [ANY],
        out_specs=VMEM,
        compiler_params=params(6),
        cost_estimate=cost(2 * 512 * 1024 * 1024, 4),
    )(*held, after)


def solve_kernel(total_ref, first_ref, second_ref, q_ref):
    pairs = ((0, 0), (0, 1), (0, 2), (1, 0), (1, 1), (2, 0))
    for slot, factor_ref in enumerate((first_ref, second_ref)):
        f = terms(factor_ref[:, :32], 3)
        z = terms(total_ref[slot], 3)
        left = jnp.concatenate([f[i] for i, _ in pairs], 1)
        right = jnp.concatenate([z[j] for _, j in pairs], 0)
        q_ref[slot] = dot(left, right, (1, 0)) * (1.0 / 128.0)


def solve(total, factors):
    return pl.pallas_call(
        solve_kernel,
        out_shape=shape(2, 32, 1024),
        in_specs=[VMEM] * 3,
        out_specs=VMEM,
        compiler_params=params(4),
        cost_estimate=cost(2 * 2 * 32 * 192 * 1024, 1),
    )(total, *factors)


def finish_kernel(side, scalars_ref, merged, lefts, q_ref, rows, error_hbm, stage, sems):
    copies, outs = [], []
    for slot, m in enumerate(members(scalars_ref, side)):
        high, low = terms(q_ref[slot], 2)
        right = jnp.concatenate([high, low, high], 0)
        for n, start in enumerate(range(0, 1024, CHUNK)):
            block = pl.ds(start, CHUNK)
            product = dot(lefts[slot][block], right, (1, 0))
            stage[slot, block] = (merged[slot][block] - product).astype(BF16)
            copy = pltpu.make_async_copy(stage.at[slot, block], error_hbm.at[0, m, block], sems.at[slot, n])
            copy.start()
            copies.append(copy)
        outs.append(dot(rows[slot][...].astype(BF16), right, (1, 0)))
    return copies, outs


def finish_own_kernel(scalars_ref, *refs):
    merged, lefts, rows, q_ref, error_hbm, out_ref, stage, sems = refs[:2], refs[2:4], refs[4:6], *refs[6:]
    copies, outs = finish_kernel(1, scalars_ref, merged, lefts, q_ref, rows, error_hbm, stage, sems)
    for slot in range(2):
        out_ref[slot] = outs[slot]
    for copy in copies:
        copy.wait()


def finish_own(scalars, merged, lefts, rows, q):
    return pl.pallas_call(
        finish_own_kernel,
        out_shape=[shape(1, 4, 1024, 1024, dtype=BF16), shape(2, 8, 1024)],
        in_specs=[SMEM] + [VMEM] * 7,
        out_specs=[HBM, VMEM],
        scratch_shapes=[pltpu.VMEM((2, 1024, 1024), BF16), pltpu.SemaphoreType.DMA((2, 1024 // CHUNK))],
        compiler_params=params(8),
        cost_estimate=cost(2 * 2 * 256 * 1024 * 1024, 4),
    )(scalars, *merged, *lefts, *rows, q)


def finish_other_kernel(scalars_ref, earlier_ref, *refs):
    merged, lefts, rows, q_ref, own_q_ref, own_rows = refs[:2], refs[2:4], refs[4:6], *refs[6:9]
    error_hbm, update_hbm, new_q_hbm, update, stage, sems, q_sems, update_sem = refs[9:]
    copies = []
    for side, source in enumerate((q_ref, own_q_ref)):
        place = pl.ds(members(scalars_ref, side)[0], 2)
        copies.append(pltpu.make_async_copy(source, new_q_hbm.at[place], q_sems.at[side]))
    for copy in copies:
        copy.start()
    more, outs = finish_kernel(0, scalars_ref, merged, lefts, q_ref, rows, error_hbm, stage, sems)
    for side, values in enumerate((outs, (own_rows[0], own_rows[1]))):
        for m, value in zip(members(scalars_ref, side), values):
            update[m] = value.astype(BF16)
    copies += [*more, pltpu.make_async_copy(update, update_hbm, update_sem)]
    copies[-1].start()
    for copy in copies:
        copy.wait()


def finish_other(scalars, error, merged, lefts, rows, q, own_q, own_rows):
    return pl.pallas_call(
        finish_other_kernel,
        out_shape=[shape(1, 4, 1024, 1024, dtype=BF16), shape(4, 8, 1024, dtype=BF16), shape(4, 32, 1024)],
        in_specs=[SMEM, HBM] + [VMEM] * 9,
        out_specs=[HBM, HBM, HBM],
        scratch_shapes=[
            pltpu.VMEM((4, 8, 1024), BF16),
            pltpu.VMEM((2, 1024, 1024), BF16),
            pltpu.SemaphoreType.DMA((2, 1024 // CHUNK)),
            pltpu.SemaphoreType.DMA((2,)),
            pltpu.SemaphoreType.DMA,
        ],
        input_output_aliases={1: 0},
        compiler_params=params(8),
        cost_estimate=cost(2 * 2 * 256 * 1024 * 1024, 4),
    )(scalars, error, *merged, *lefts, *rows, q, own_q, own_rows)


def add_kernel(count, scale, *refs):
    values = [ref[...] for ref in refs[:count]]
    while len(values) > 1:
        values = [values[n] + values[n + 1] for n in range(0, len(values), 2)]
    refs[-1][...] = values[0] * scale


def add(values, after=(), scale=1.0):
    return pl.pallas_call(
        lambda *refs: add_kernel(len(values), scale, *refs),
        out_shape=shape(2, 32, 1024),
        in_specs=[VMEM] * len(values) + [ANY] * len(after),
        out_specs=VMEM,
        compiler_params=params(4),
        cost_estimate=cost(65536, 0.375),
    )(*values, *after)


def received(step, value):
    return [lax.ppermute(value, AXES, step_pairs(step, mask)) for mask in (1, 3, 2)]


def on_device(inputs, cotangents, error_buffer, previous_q):
    scalars = jnp.stack([lax.axis_index("row") % 2, lax.axis_index(AXES)]).astype(jnp.int32)
    arrays = [pltpu.with_memory_space_constraint(a, pltpu.HBM) for a in (inputs, cotangents, error_buffer, previous_q)]
    *other_held, other = load(0, scalars, arrays)
    *own_held, own = load(1, scalars, arrays)
    total = add([own, other_core(other)])
    merged = {}
    for step in range(3):
        came = received(step, total)
        fill = []
        if step < 2:
            fill = [merge(slot, other_held if step else own_held, total) for slot in range(2)]
            merged[1 - step] = fill
        total = add([total, *came], fill, 1.0 / 128.0 if step == 2 else 1.0)
    mean = total
    other_mean = other_core(mean)
    own = project(own_held, mean, mean)
    other = project(other_held, other_mean, own)
    total = add([own, other_core(other)])
    for step in range(3):
        came = received(step, total)
        fill = []
        if step == 0:
            solved = [gram_schmidt(slot, mean, total) for slot in range(2)]
            basis, factors = zip(*solved)
            other_basis = [other_core(b) for b in basis]
            fill = list(basis)
        elif step == 1:
            own_flip, other_flip = flip(scalars, basis, total), flip(scalars, other_basis, total)
            fill = [own_flip[0], other_flip[0]]
        total = add([total, *came], fill)
    own_q = solve(total, factors)
    other_q = other_core(own_q)
    error, own_rows = finish_own(scalars, merged[1], own_flip[:2], own_flip[2:], own_q)
    return finish_other(scalars, error, merged[0], other_flip[:2], other_flip[2:], other_q, own_q, own_rows)


def solution(mesh):
    return jax.shard_map(
        on_device,
        mesh=mesh,
        in_specs=(
            P(None, AXES, None),
            P(None, AXES, None),
            P(AXES, None, None, None),
            P(),
        ),
        out_specs=(P(AXES, None, None, None), P(None, AXES, None), P()),
        check_vma=False,
    )
```

time: 111 us -> 91.9 us (0.83)
  starting transfers between devices: 52.1 us -> 31.6 us
  waiting for transfers between devices: 19.7 us -> 24.6 us
  Pallas kernels: 37.8 us -> 34.5 us
    ppermute x24 -> x18, starting transfers between devices: 33.8 us -> 22.4 us  [received(): lax.ppermute(value, AXES, step_pairs(step, mask))]
    ppermute x10 -> x6, starting transfers between devices: 18.3 us -> 9.28 us  [other_core(): return lax.ppermute(value, AXES, core_pairs())]
    ppermute x24 -> x18, waiting for transfers between devices: 18.7 us -> 23 us  [received(): lax.ppermute(value, AXES, step_pairs(step, mask))]
    pallas_call x12 -> x17, Pallas kernels: 30.1 us -> 26.8 us  [the longest x2 10.2 us: load(): pl.pallas_call(lambda *refs: load_kernel(side, *refs), out_shape=[pltpu.V...]
  transfers between devices with their start and end apart: 34 -> 24, of which waited for: 12 -> 14; matrix products, arithmetic and copies ran while one was open for 0% -> 0% of each run, Pallas kernels for 19% -> 26%
where the time goes in v2:
time: 91.9 us; the launch traced here: 91.8 us
  Pallas kernels  34.5 us (38%)
  starting transfers between devices  31.6 us (34%)
  waiting for transfers between devices  24.6 us (27%)
  between operations  1.03 us (1%)
    ppermute x18, waiting for transfers between devices, received(): lax.ppermute(value, AXES, step_pairs(step, mask))  23 us
    ppermute x18, starting transfers between devices, received(): lax.ppermute(value, AXES, step_pairs(step, mask))  22.4 us
    pallas_call x2, Pallas kernels, load(): pl.pallas_call(lambda *refs: load_kernel(side, *refs), out_shape=[pltpu.V...  10.2 us
    ppermute x6, starting transfers between devices, other_core(): return lax.ppermute(value, AXES, core_pairs())  9.28 us
    pallas_call x2, Pallas kernels, gram_schmidt(): pl.pallas_call(lambda *refs: gram_schmidt_kernel(slot, *refs), out_shape=...  6.34 us
    pallas_call x4, Pallas kernels, merge(): pl.pallas_call(lambda *refs: merge_kernel(slot, *refs), out_shape=pltpu.V...  5.22 us
    pallas_call x2, Pallas kernels, project(): pl.pallas_call(project_kernel, out_shape=shape(2, 32, 1024), in_specs=[VM...  3.53 us
    pallas_call x1, Pallas kernels, finish_other(): pl.pallas_call(finish_other_kernel, out_shape=[shape(1, 4, 1024, 1024, dt...  3.1 us
  transfers between devices with their start and end apart: 24, of which 14 were waited for; matrix products, arithmetic and copies ran while one was open for 0% of the time, Pallas kernels for 26%

profile of v2, /device:TPU:1, one launch (start us, length us, event | category | flops | bytes accessed | tf_op | source)
XLA Modules:
  0.0 91.8 jit_solution(7556881566286157443)
XLA Ops:
  0.7 5.1 %shard_map.68 = (bf16[2,512,1024]{2,1,0:T(8,128)(2,1)S(1)}, bf16[2,512,1024]{2,1,0:T(8,128)(2,1)S(1)}, bf16[2,1024,1024]{2,1,0:T(8,128)(2,1)S(1)}, f32[2,32,1024]{2,1,0:T(8,128)S(1)}) custom-call(s32[2]{0:T(128)S(1)} %pad_add_fusion.refs_0_.scalars_ref, bf16[4,512,1024]{2,1,0:T(8,128)(2,1)} %refs_1_.3, bf16[4,512,1024]{2,1,0:T(8,128)(2,1)} %refs_2_.3, ...), custom_call_target="tpu_custom_call" | custom-call | flops 805306368 | bytes 9437184 | tf_op jit(solution)/shard_map/pallas_call | solution.py:136
  5.8 1.5 %collective-permute-start = (f32[2,32,1024]{2,1,0:T(8,128)S(1)}, f32[2,32,1024]{2,1,0:T(8,128)S(1)}, u32[]{:S(2)}, u32[]{:S(2)}) collective-permute-start(f32[2,32,1024]{2,1,0:T(8,128)S(1)} %get-tuple-element.29), channel_id=1, source_target_pairs={{0,8},{1,9},{2,10},{3,11},{4,12},{5,13},{6,14},{7,15},{8,0},{9,1},... | collective-permute-start | bytes 786440 | tf_op jit(solution)/shard_map/ppermute | solution.py:52
  7.3 5.1 %shard_map.67 = (bf16[2,512,1024]{2,1,0:T(8,128)(2,1)S(1)}, bf16[2,512,1024]{2,1,0:T(8,128)(2,1)S(1)}, bf16[2,1024,1024]{2,1,0:T(8,128)(2,1)S(1)}, f32[2,32,1024]{2,1,0:T(8,128)S(1)}) custom-call(s32[2]{0:T(128)S(1)} %pad_add_fusion.refs_0_.scalars_ref, bf16[4,512,1024]{2,1,0:T(8,128)(2,1)} %refs_1_.3, bf16[4,512,1024]{2,1,0:T(8,128)(2,1)} %refs_2_.3, ...), custom_call_target="tpu_custom_call" | custom-call | flops 805306368 | bytes 9437184 | tf_op jit(solution)/shard_map/pallas_call | solution.py:136
  12.5 3.1 %collective-permute-start.3 = (f32[2,32,1024]{2,1,0:T(8,128)S(1)}, f32[2,32,1024]{2,1,0:T(8,128)S(1)}, u32[]{:S(2)}, u32[]{:S(2)}) collective-permute-start(f32[2,32,1024]{2,1,0:T(8,128)S(1)} %shard_map.69.refs_3_.refs_0_), channel_id=1, source_target_pairs={{0,4},{1,5},{2,6},{3,7},{4,0},{5,1},{6,2},{7,3},{8,40},{9,41},{10,... | collective-permute-start | bytes 786440 | tf_op jit(solution)/shard_map/ppermute | solution.py:357
  19.7 2.8 %collective-permute-done.2.refs_2_ = f32[2,32,1024]{2,1,0:T(8,128)S(1)} collective-permute-done((f32[2,32,1024]{2,1,0:T(8,128)S(1)}, f32[2,32,1024]{2,1,0:T(8,128)S(1)}, u32[]{:S(2)}, u32[]{:S(2)}) %collective-permute-start.2) | collective-permute-done | bytes 262176 | tf_op jit(solution)/shard_map/ppermute | solution.py:357
  23.0 3.7 %collective-permute-start.6 = (f32[2,32,1024]{2,1,0:T(8,128)S(1)}, f32[2,32,1024]{2,1,0:T(8,128)S(1)}, u32[]{:S(2)}, u32[]{:S(2)}) collective-permute-start(f32[2,32,1024]{2,1,0:T(8,128)S(1)} %shard_map.72.refs_3_.refs_0_), channel_id=1, source_target_pairs={{0,32},{1,33},{2,34},{3,35},{4,36},{5,37},{6,38},{7,39},{8,72},{9,... | collective-permute-start | bytes 786440 | tf_op jit(solution)/shard_map/ppermute | solution.py:357
  27.4 1.3 %shard_map.74.refs_5_.refs_1_ = f32[1024,1024]{1,0:T(8,128)S(1)} custom-call(bf16[2,512,1024]{2,1,0:T(8,128)(2,1)S(1)} %get-tuple-element.30.refs_0_.x_ref, bf16[2,512,1024]{2,1,0:T(8,128)(2,1)S(1)} %get-tuple-element.31.refs_1_.c_ref, bf16[2,1024,1024]{2,1,0:T(8,128)(2,1)S(1)} %get-tuple-element.32.refs_2_.e_ref, f32[2,32,1024]{2,1,0:T(8,128)S(1)} %shard_map.72.refs_3_.refs_0_), custom_call_target="tpu_custom_call" | custom-call | flops 1073741824 | bytes 4194304 | tf_op jit(solution)/shard_map/pallas_call | solution.py:232
  28.7 1.3 %shard_map.73.refs_4_.refs_0_ = f32[1024,1024]{1,0:T(8,128)S(1)} custom-call(bf16[2,512,1024]{2,1,0:T(8,128)(2,1)S(1)} %get-tuple-element.30.refs_0_.x_ref, bf16[2,512,1024]{2,1,0:T(8,128)(2,1)S(1)} %get-tuple-element.31.refs_1_.c_ref, bf16[2,1024,1024]{2,1,0:T(8,128)(2,1)S(1)} %get-tuple-element.32.refs_2_.e_ref, f32[2,32,1024]{2,1,0:T(8,128)S(1)} %shard_map.72.refs_3_.refs_0_), custom_call_target="tpu_custom_call" | custom-call | flops 1073741824 | bytes 4194304 | tf_op jit(solution)/shard_map/pallas_call | solution.py:232
  30.7 2.8 %collective-permute-done.5.refs_2_ = f32[2,32,1024]{2,1,0:T(8,128)S(1)} collective-permute-done((f32[2,32,1024]{2,1,0:T(8,128)S(1)}, f32[2,32,1024]{2,1,0:T(8,128)S(1)}, u32[]{:S(2)}, u32[]{:S(2)}) %collective-permute-start.5) | collective-permute-done | bytes 262176 | tf_op jit(solution)/shard_map/ppermute | solution.py:357
  34.3 2.2 %collective-permute-start.9 = (f32[2,32,1024]{2,1,0:T(8,128)S(1)}, f32[2,32,1024]{2,1,0:T(8,128)S(1)}, u32[]{:S(2)}, u32[]{:S(2)}) collective-permute-start(f32[2,32,1024]{2,1,0:T(8,128)S(1)} %shard_map.75.refs_0_), channel_id=1, source_target_pairs={{0,64},{1,65},{2,66},{3,67},{4,68},{5,69},{6,70},{7,71},{8,12},{9,... | collective-permute-start | bytes 786440 | tf_op jit(solution)/shard_map/ppermute | solution.py:357
  36.6 1.5 %collective-permute-start.8 = (f32[2,32,1024]{2,1,0:T(8,128)S(1)}, f32[2,32,1024]{2,1,0:T(8,128)S(1)}, u32[]{:S(2)}, u32[]{:S(2)}) collective-permute-start(f32[2,32,1024]{2,1,0:T(8,128)S(1)} %shard_map.75.refs_0_), channel_id=1, source_target_pairs={{0,65},{1,64},{2,67},{3,66},{4,69},{5,68},{6,71},{7,70},{8,14},{9,... | collective-permute-start | bytes 786440 | tf_op jit(solution)/shard_map/ppermute | solution.py:357
  38.0 3.4 %collective-permute-done.9.refs_3_ = f32[2,32,1024]{2,1,0:T(8,128)S(1)} collective-permute-done((f32[2,32,1024]{2,1,0:T(8,128)S(1)}, f32[2,32,1024]{2,1,0:T(8,128)S(1)}, u32[]{:S(2)}, u32[]{:S(2)}) %collective-permute-start.9) | collective-permute-done | bytes 262176 | tf_op jit(solution)/shard_map/ppermute | solution.py:357
  41.4 2.8 %collective-permute-done.8.refs_2_ = f32[2,32,1024]{2,1,0:T(8,128)S(1)} collective-permute-done((f32[2,32,1024]{2,1,0:T(8,128)S(1)}, f32[2,32,1024]{2,1,0:T(8,128)S(1)}, u32[]{:S(2)}, u32[]{:S(2)}) %collective-permute-start.8) | collective-permute-done | bytes 262176 | tf_op jit(solution)/shard_map/ppermute | solution.py:357
  44.3 2.9 %collective-permute-start.10 = (f32[2,32,1024]{2,1,0:T(8,128)S(1)}, f32[2,32,1024]{2,1,0:T(8,128)S(1)}, u32[]{:S(2)}, u32[]{:S(2)}) collective-permute-start(f32[2,32,1024]{2,1,0:T(8,128)S(1)} %shard_map.76.p_ref.after_ref.refs_0_), channel_id=1, source_target_pairs={{0,8},{1,9},{2,10},{3,11},{4,12},{5,13},{6,14},{7,15},{8,0},{9,1},... | collective-permute-start | bytes 786440 | tf_op jit(solution)/shard_map/ppermute | solution.py:52
  47.2 1.8 %shard_map.77.after_ref.refs_0_ = f32[2,32,1024]{2,1,0:T(8,128)S(1)} custom-call(bf16[2,512,1024]{2,1,0:T(8,128)(2,1)S(1)} %get-tuple-element.25.refs_0_.x_ref, bf16[2,512,1024]{2,1,0:T(8,128)(2,1)S(1)} %get-tuple-element.26.refs_1_.c_ref, bf16[2,1024,1024]{2,1,0:T(8,128)(2,1)S(1)} %get-tuple-element.27.refs_2_.e_ref, ...), custom_call_target="tpu_custom_call" | custom-call | flops 805306368 | bytes 8388608 | tf_op jit(solution)/shard_map/pallas_call | solution.py:160
  49.0 1.8 %shard_map.78 = f32[2,32,1024]{2,1,0:T(8,128)S(1)} custom-call(bf16[2,512,1024]{2,1,0:T(8,128)(2,1)S(1)} %get-tuple-element.30.refs_0_.x_ref, bf16[2,512,1024]{2,1,0:T(8,128)(2,1)S(1)} %get-tuple-element.31.refs_1_.c_ref, bf16[2,1024,1024]{2,1,0:T(8,128)(2,1)S(1)} %get-tuple-element.32.refs_2_.e_ref, f32[2,32,1024]{2,1,0:T(8,128)S(1)} %collective-permute-done.10.p_ref, ...), custom_call_target="tpu_custom_call" | custom-call | flops 805306368 | bytes 8388608 | tf_op jit(solution)/shard_map/pallas_call | solution.py:160
  50.8 1.5 %collective-permute-done.11.refs_1_ = f32[2,32,1024]{2,1,0:T(8,128)S(1)} collective-permute-done((f32[2,32,1024]{2,1,0:T(8,128)S(1)}, f32[2,32,1024]{2,1,0:T(8,128)S(1)}, u32[]{:S(2)}, u32[]{:S(2)}) %collective-permute-start.11) | collective-permute-done | bytes 262176 | tf_op jit(solution)/shard_map/ppermute | solution.py:52
  52.4 1.8 %collective-permute-start.14 = (f32[2,32,1024]{2,1,0:T(8,128)S(1)}, f32[2,32,1024]{2,1,0:T(8,128)S(1)}, u32[]{:S(2)}, u32[]{:S(2)}) collective-permute-start(f32[2,32,1024]{2,1,0:T(8,128)S(1)} %shard_map.79.refs_1_.refs_0_), channel_id=1, source_target_pairs={{0,4},{1,5},{2,6},{3,7},{4,0},{5,1},{6,2},{7,3},{8,40},{9,41},{10,... | collective-permute-start | bytes 786440 | tf_op jit(solution)/shard_map/ppermute | solution.py:357
  54.2 1.7 %collective-permute-start.13 = (f32[2,32,1024]{2,1,0:T(8,128)S(1)}, f32[2,32,1024]{2,1,0:T(8,128)S(1)}, u32[]{:S(2)}, u32[]{:S(2)}) collective-permute-start(f32[2,32,1024]{2,1,0:T(8,128)S(1)} %shard_map.79.refs_1_.refs_0_), channel_id=1, source_target_pairs={{0,6},{1,7},{2,4},{3,5},{4,2},{5,3},{6,0},{7,1},{8,56},{9,57},{10,... | collective-permute-start | bytes 786440 | tf_op jit(solution)/shard_map/ppermute | solution.py:357
  55.9 3.2 %shard_map.81 = (f32[32,1024]{1,0:T(8,128)S(1)}, f32[32,128]{1,0:T(8,128)S(1)}) custom-call(f32[2,32,1024]{2,1,0:T(8,128)S(1)} %shard_map.76.p_ref.after_ref.refs_0_, f32[2,32,1024]{2,1,0:T(8,128)S(1)} %shard_map.79.refs_1_.refs_0_), custom_call_target="tpu_custom_call" | custom-call | flops 4000000 | bytes 8388608 | tf_op jit(solution)/shard_map/pallas_call | solution.py:192
  59.1 3.2 %shard_map.80 = (f32[32,1024]{1,0:T(8,128)S(1)}, f32[32,128]{1,0:T(8,128)S(1)}) custom-call(f32[2,32,1024]{2,1,0:T(8,128)S(1)} %shard_map.76.p_ref.after_ref.refs_0_, f32[2,32,1024]{2,1,0:T(8,128)S(1)} %shard_map.79.refs_1_.refs_0_), custom_call_target="tpu_custom_call" | custom-call | flops 4000000 | bytes 8388608 | tf_op jit(solution)/shard_map/pallas_call | solution.py:192
  62.4 1.8 %collective-permute-start.17 = (f32[2,32,1024]{2,1,0:T(8,128)S(1)}, f32[2,32,1024]{2,1,0:T(8,128)S(1)}, u32[]{:S(2)}, u32[]{:S(2)}) collective-permute-start(f32[2,32,1024]{2,1,0:T(8,128)S(1)} %shard_map.82.after_ref.refs_0_), channel_id=1, source_target_pairs={{0,32},{1,33},{2,34},{3,35},{4,36},{5,37},{6,38},{7,39},{8,72},{9,... | collective-permute-start | bytes 786440 | tf_op jit(solution)/shard_map/ppermute | solution.py:357
  64.2 1.4 %collective-permute-start.16 = (f32[2,32,1024]{2,1,0:T(8,128)S(1)}, f32[2,32,1024]{2,1,0:T(8,128)S(1)}, u32[]{:S(2)}, u32[]{:S(2)}) collective-permute-start(f32[2,32,1024]{2,1,0:T(8,128)S(1)} %shard_map.82.after_ref.refs_0_), channel_id=1, source_target_pairs={{0,48},{1,49},{2,50},{3,51},{4,52},{5,53},{6,54},{7,55},{8,73},{9,... | collective-permute-start | bytes 786440 | tf_op jit(solution)/shard_map/ppermute | solution.py:357
  65.6 1.9 %collective-permute-start.19 = (f32[32,1024]{1,0:T(8,128)S(1)}, f32[32,1024]{1,0:T(8,128)S(1)}, u32[]{:S(2)}, u32[]{:S(2)}) collective-permute-start(f32[32,1024]{1,0:T(8,128)S(1)} %get-tuple-element.34.refs_5_.second_ref), channel_id=1, source_target_pairs={{0,8},{1,9},{2,10},{3,11},{4,12},{5,13},{6,14},{7,15},{8,0},{9,1},... | collective-permute-start | bytes 393224 | tf_op jit(solution)/shard_map/ppermute | solution.py:52
  70.1 2.2 %collective-permute-done.16.refs_2_ = f32[2,32,1024]{2,1,0:T(8,128)S(1)} collective-permute-done((f32[2,32,1024]{2,1,0:T(8,128)S(1)}, f32[2,32,1024]{2,1,0:T(8,128)S(1)}, u32[]{:S(2)}, u32[]{:S(2)}) %collective-permute-start.16) | collective-permute-done | bytes 262176 | tf_op jit(solution)/shard_map/ppermute | solution.py:357
  72.4 1.9 %collective-permute-start.22 = (f32[2,32,1024]{2,1,0:T(8,128)S(1)}, f32[2,32,1024]{2,1,0:T(8,128)S(1)}, u32[]{:S(2)}, u32[]{:S(2)}) collective-permute-start(f32[2,32,1024]{2,1,0:T(8,128)S(1)} %shard_map.85.refs_0_), channel_id=1, source_target_pairs={{0,64},{1,65},{2,66},{3,67},{4,68},{5,69},{6,70},{7,71},{8,12},{9,... | collective-permute-start | bytes 786440 | tf_op jit(solution)/shard_map/ppermute | solution.py:357
  74.2 1.8 %collective-permute-start.21 = (f32[2,32,1024]{2,1,0:T(8,128)S(1)}, f32[2,32,1024]{2,1,0:T(8,128)S(1)}, u32[]{:S(2)}, u32[]{:S(2)}) collective-permute-start(f32[2,32,1024]{2,1,0:T(8,128)S(1)} %shard_map.85.refs_0_), channel_id=1, source_target_pairs={{0,65},{1,64},{2,67},{3,66},{4,69},{5,68},{6,71},{7,70},{8,14},{9,... | collective-permute-start | bytes 786440 | tf_op jit(solution)/shard_map/ppermute | solution.py:357
  76.0 3.4 %collective-permute-done.22.refs_3_ = f32[2,32,1024]{2,1,0:T(8,128)S(1)} collective-permute-done((f32[2,32,1024]{2,1,0:T(8,128)S(1)}, f32[2,32,1024]{2,1,0:T(8,128)S(1)}, u32[]{:S(2)}, u32[]{:S(2)}) %collective-permute-start.22) | collective-permute-done | bytes 262176 | tf_op jit(solution)/shard_map/ppermute | solution.py:357
  79.5 2.8 %collective-permute-done.21.refs_2_ = f32[2,32,1024]{2,1,0:T(8,128)S(1)} collective-permute-done((f32[2,32,1024]{2,1,0:T(8,128)S(1)}, f32[2,32,1024]{2,1,0:T(8,128)S(1)}, u32[]{:S(2)}, u32[]{:S(2)}) %collective-permute-start.21) | collective-permute-done | bytes 262176 | tf_op jit(solution)/shard_map/ppermute | solution.py:357
  82.7 3.0 %collective-permute-start.23 = (f32[2,32,1024]{2,1,0:T(8,128)S(1)}, f32[2,32,1024]{2,1,0:T(8,128)S(1)}, u32[]{:S(2)}, u32[]{:S(2)}) collective-permute-start(f32[2,32,1024]{2,1,0:T(8,128)S(1)} %shard_map.87.refs_6_.refs_7_), channel_id=1, source_target_pairs={{0,8},{1,9},{2,10},{3,11},{4,12},{5,13},{6,14},{7,15},{8,0},{9,1},... | collective-permute-start | bytes 786440 | tf_op jit(solution)/shard_map/ppermute | solution.py:52
  85.6 2.9 %shard_map.88 = (bf16[1,4,1024,1024]{3,2,1,0:T(8,128)(2,1)}, f32[2,8,1024]{2,1,0:T(8,128)S(1)}) custom-call(s32[2]{0:T(128)S(1)} %pad_add_fusion.refs_0_.scalars_ref, f32[1024,1024]{1,0:T(8,128)S(1)} %shard_map.70.refs_4_.refs_0_, f32[1024,1024]{1,0:T(8,128)S(1)} %shard_map.71.refs_5_.refs_1_, bf16[1024,96]{1,0:T(8,128)(2,1)S(1)} %get-tuple-element.35.refs_4_.refs_2_, ...), custom_call_target="tpu_custom_call" | custom-call | flops 1073741824 | bytes 4194304 | tf_op jit(solution)/shard_map/pallas_call | solution.py:289
  88.5 3.1 %shard_map.89 = (bf16[1,4,1024,1024]{3,2,1,0:T(8,128)(2,1)}, bf16[4,8,1024]{2,1,0:T(8,128)(2,1)}, f32[4,32,1024]{2,1,0:T(8,128)}) custom-call(s32[2]{0:T(128)S(1)} %pad_add_fusion.refs_0_.scalars_ref, bf16[1,4,1024,1024]{3,2,1,0:T(8,128)(2,1)} %get-tuple-element.42.earlier_ref, ...), custom_call_target="tpu_custom_call", output_to_operand_aliasing={{0}: (1, {})} | custom-call | flops 1073741824 | bytes 4194304 | tf_op jit(solution)/shard_map/pallas_call | solution.py:320
  (40 shorter events, 10.1 us)
Async XLA Ops:
  5.8 6.6 %collective-permute-start = (f32[2,32,1024]{2,1,0:T(8,128)S(1)}, f32[2,32,1024]{2,1,0:T(8,128)S(1)}, u32[]{:S(2)}, u32[]{:S(2)}) collective-permute-start(f32[2,32,1024]{2,1,0:T(8,128)S(1)} %get-tuple-element.29), channel_id=1, source_target_pairs={{0,8},{1,9},{2,10},{3,11},{4,12},{5,13},{6,14},{7,15},{8,0},{9,1},... | collective-permute-start | bytes 786440 | tf_op jit(solution)/shard_map/ppermute | solution.py:52
  12.5 7.1 %collective-permute-start.3 = (f32[2,32,1024]{2,1,0:T(8,128)S(1)}, f32[2,32,1024]{2,1,0:T(8,128)S(1)}, u32[]{:S(2)}, u32[]{:S(2)}) collective-permute-start(f32[2,32,1024]{2,1,0:T(8,128)S(1)} %shard_map.69.refs_3_.refs_0_), channel_id=1, source_target_pairs={{0,4},{1,5},{2,6},{3,7},{4,0},{5,1},{6,2},{7,3},{8,40},{9,41},{10,... | collective-permute-start | bytes 786440 | tf_op jit(solution)/shard_map/ppermute | solution.py:357
  15.6 6.9 %collective-permute-start.2 = (f32[2,32,1024]{2,1,0:T(8,128)S(1)}, f32[2,32,1024]{2,1,0:T(8,128)S(1)}, u32[]{:S(2)}, u32[]{:S(2)}) collective-permute-start(f32[2,32,1024]{2,1,0:T(8,128)S(1)} %shard_map.69.refs_3_.refs_0_), channel_id=1, source_target_pairs={{0,6},{1,7},{2,4},{3,5},{4,2},{5,3},{6,0},{7,1},{8,56},{9,57},{10,... | collective-permute-start | bytes 786440 | tf_op jit(solution)/shard_map/ppermute | solution.py:357
  16.4 6.5 %collective-permute-start.1 = (f32[2,32,1024]{2,1,0:T(8,128)S(1)}, f32[2,32,1024]{2,1,0:T(8,128)S(1)}, u32[]{:S(2)}, u32[]{:S(2)}) collective-permute-start(f32[2,32,1024]{2,1,0:T(8,128)S(1)} %shard_map.69.refs_3_.refs_0_), channel_id=1, source_target_pairs={{0,2},{1,3},{2,0},{3,1},{4,6},{5,7},{6,4},{7,5},{8,24},{9,25},{10,... | collective-permute-start | bytes 786440 | tf_op jit(solution)/shard_map/ppermute | solution.py:357
  23.0 7.7 %collective-permute-start.6 = (f32[2,32,1024]{2,1,0:T(8,128)S(1)}, f32[2,32,1024]{2,1,0:T(8,128)S(1)}, u32[]{:S(2)}, u32[]{:S(2)}) collective-permute-start(f32[2,32,1024]{2,1,0:T(8,128)S(1)} %shard_map.72.refs_3_.refs_0_), channel_id=1, source_target_pairs={{0,32},{1,33},{2,34},{3,35},{4,36},{5,37},{6,38},{7,39},{8,72},{9,... | collective-permute-start | bytes 786440 | tf_op jit(solution)/shard_map/ppermute | solution.py:357
  26.6 6.9 %collective-permute-start.5 = (f32[2,32,1024]{2,1,0:T(8,128)S(1)}, f32[2,32,1024]{2,1,0:T(8,128)S(1)}, u32[]{:S(2)}, u32[]{:S(2)}) collective-permute-start(f32[2,32,1024]{2,1,0:T(8,128)S(1)} %shard_map.72.refs_3_.refs_0_), channel_id=1, source_target_pairs={{0,48},{1,49},{2,50},{3,51},{4,52},{5,53},{6,54},{7,55},{8,73},{9,... | collective-permute-start | bytes 786440 | tf_op jit(solution)/shard_map/ppermute | solution.py:357
  27.1 7.2 %collective-permute-start.4 = (f32[2,32,1024]{2,1,0:T(8,128)S(1)}, f32[2,32,1024]{2,1,0:T(8,128)S(1)}, u32[]{:S(2)}, u32[]{:S(2)}) collective-permute-start(f32[2,32,1024]{2,1,0:T(8,128)S(1)} %shard_map.72.refs_3_.refs_0_), channel_id=1, source_target_pairs={{0,16},{1,17},{2,18},{3,19},{4,20},{5,21},{6,22},{7,23},{8,9},{9,8... | collective-permute-start | bytes 786440 | tf_op jit(solution)/shard_map/ppermute | solution.py:357
  34.3 7.1 %collective-permute-start.9 = (f32[2,32,1024]{2,1,0:T(8,128)S(1)}, f32[2,32,1024]{2,1,0:T(8,128)S(1)}, u32[]{:S(2)}, u32[]{:S(2)}) collective-permute-start(f32[2,32,1024]{2,1,0:T(8,128)S(1)} %shard_map.75.refs_0_), channel_id=1, source_target_pairs={{0,64},{1,65},{2,66},{3,67},{4,68},{5,69},{6,70},{7,71},{8,12},{9,... | collective-permute-start | bytes 786440 | tf_op jit(solution)/shard_map/ppermute | solution.py:357
  36.6 7.7 %collective-permute-start.8 = (f32[2,32,1024]{2,1,0:T(8,128)S(1)}, f32[2,32,1024]{2,1,0:T(8,128)S(1)}, u32[]{:S(2)}, u32[]{:S(2)}) collective-permute-start(f32[2,32,1024]{2,1,0:T(8,128)S(1)} %shard_map.75.refs_0_), channel_id=1, source_target_pairs={{0,65},{1,64},{2,67},{3,66},{4,69},{5,68},{6,71},{7,70},{8,14},{9,... | collective-permute-start | bytes 786440 | tf_op jit(solution)/shard_map/ppermute | solution.py:357
  38.0 6.3 %collective-permute-start.7 = (f32[2,32,1024]{2,1,0:T(8,128)S(1)}, f32[2,32,1024]{2,1,0:T(8,128)S(1)}, u32[]{:S(2)}, u32[]{:S(2)}) collective-permute-start(f32[2,32,1024]{2,1,0:T(8,128)S(1)} %shard_map.75.refs_0_), channel_id=1, source_target_pairs={{0,1},{1,0},{2,3},{3,2},{4,5},{5,4},{6,7},{7,6},{8,10},{9,11},{10,... | collective-permute-start | bytes 786440 | tf_op jit(solution)/shard_map/ppermute | solution.py:357
  44.3 4.7 %collective-permute-start.10 = (f32[2,32,1024]{2,1,0:T(8,128)S(1)}, f32[2,32,1024]{2,1,0:T(8,128)S(1)}, u32[]{:S(2)}, u32[]{:S(2)}) collective-permute-start(f32[2,32,1024]{2,1,0:T(8,128)S(1)} %shard_map.76.p_ref.after_ref.refs_0_), channel_id=1, source_target_pairs={{0,8},{1,9},{2,10},{3,11},{4,12},{5,13},{6,14},{7,15},{8,0},{9,1},... | collective-permute-start | bytes 786440 | tf_op jit(solution)/shard_map/ppermute | solution.py:52
  50.8 1.6 %collective-permute-start.11 = (f32[2,32,1024]{2,1,0:T(8,128)S(1)}, f32[2,32,1024]{2,1,0:T(8,128)S(1)}, u32[]{:S(2)}, u32[]{:S(2)}) collective-permute-start(f32[2,32,1024]{2,1,0:T(8,128)S(1)} %shard_map.78), channel_id=1, source_target_pairs={{0,8},{1,9},{2,10},{3,11},{4,12},{5,13},{6,14},{7,15},{8,0},{9,1},... | collective-permute-start | bytes 786440 | tf_op jit(solution)/shard_map/ppermute | solution.py:52
  52.4 9.9 %collective-permute-start.14 = (f32[2,32,1024]{2,1,0:T(8,128)S(1)}, f32[2,32,1024]{2,1,0:T(8,128)S(1)}, u32[]{:S(2)}, u32[]{:S(2)}) collective-permute-start(f32[2,32,1024]{2,1,0:T(8,128)S(1)} %shard_map.79.refs_1_.refs_0_), channel_id=1, source_target_pairs={{0,4},{1,5},{2,6},{3,7},{4,0},{5,1},{6,2},{7,3},{8,40},{9,41},{10,... | collective-permute-start | bytes 786440 | tf_op jit(solution)/shard_map/ppermute | solution.py:357
  54.2 8.1 %collective-permute-start.13 = (f32[2,32,1024]{2,1,0:T(8,128)S(1)}, f32[2,32,1024]{2,1,0:T(8,128)S(1)}, u32[]{:S(2)}, u32[]{:S(2)}) collective-permute-start(f32[2,32,1024]{2,1,0:T(8,128)S(1)} %shard_map.79.refs_1_.refs_0_), channel_id=1, source_target_pairs={{0,6},{1,7},{2,4},{3,5},{4,2},{5,3},{6,0},{7,1},{8,56},{9,57},{10,... | collective-permute-start | bytes 786440 | tf_op jit(solution)/shard_map/ppermute | solution.py:357
  55.9 6.4 %collective-permute-start.12 = (f32[2,32,1024]{2,1,0:T(8,128)S(1)}, f32[2,32,1024]{2,1,0:T(8,128)S(1)}, u32[]{:S(2)}, u32[]{:S(2)}) collective-permute-start(f32[2,32,1024]{2,1,0:T(8,128)S(1)} %shard_map.79.refs_1_.refs_0_), channel_id=1, source_target_pairs={{0,2},{1,3},{2,0},{3,1},{4,6},{5,7},{6,4},{7,5},{8,24},{9,25},{10,... | collective-permute-start | bytes 786440 | tf_op jit(solution)/shard_map/ppermute | solution.py:357
  62.4 7.7 %collective-permute-start.17 = (f32[2,32,1024]{2,1,0:T(8,128)S(1)}, f32[2,32,1024]{2,1,0:T(8,128)S(1)}, u32[]{:S(2)}, u32[]{:S(2)}) collective-permute-start(f32[2,32,1024]{2,1,0:T(8,128)S(1)} %shard_map.82.after_ref.refs_0_), channel_id=1, source_target_pairs={{0,32},{1,33},{2,34},{3,35},{4,36},{5,37},{6,38},{7,39},{8,72},{9,... | collective-permute-start | bytes 786440 | tf_op jit(solution)/shard_map/ppermute | solution.py:357
  64.2 8.1 %collective-permute-start.16 = (f32[2,32,1024]{2,1,0:T(8,128)S(1)}, f32[2,32,1024]{2,1,0:T(8,128)S(1)}, u32[]{:S(2)}, u32[]{:S(2)}) collective-permute-start(f32[2,32,1024]{2,1,0:T(8,128)S(1)} %shard_map.82.after_ref.refs_0_), channel_id=1, source_target_pairs={{0,48},{1,49},{2,50},{3,51},{4,52},{5,53},{6,54},{7,55},{8,73},{9,... | collective-permute-start | bytes 786440 | tf_op jit(solution)/shard_map/ppermute | solution.py:357
  65.6 6.7 %collective-permute-start.15 = (f32[2,32,1024]{2,1,0:T(8,128)S(1)}, f32[2,32,1024]{2,1,0:T(8,128)S(1)}, u32[]{:S(2)}, u32[]{:S(2)}) collective-permute-start(f32[2,32,1024]{2,1,0:T(8,128)S(1)} %shard_map.82.after_ref.refs_0_), channel_id=1, source_target_pairs={{0,16},{1,17},{2,18},{3,19},{4,20},{5,21},{6,22},{7,23},{8,9},{9,8... | collective-permute-start | bytes 786440 | tf_op jit(solution)/shard_map/ppermute | solution.py:357
  65.6 3.1 %collective-permute-start.19 = (f32[32,1024]{1,0:T(8,128)S(1)}, f32[32,1024]{1,0:T(8,128)S(1)}, u32[]{:S(2)}, u32[]{:S(2)}) collective-permute-start(f32[32,1024]{1,0:T(8,128)S(1)} %get-tuple-element.34.refs_5_.second_ref), channel_id=1, source_target_pairs={{0,8},{1,9},{2,10},{3,11},{4,12},{5,13},{6,14},{7,15},{8,0},{9,1},... | collective-permute-start | bytes 393224 | tf_op jit(solution)/shard_map/ppermute | solution.py:52
  67.5 1.3 %collective-permute-start.18 = (f32[32,1024]{1,0:T(8,128)S(1)}, f32[32,1024]{1,0:T(8,128)S(1)}, u32[]{:S(2)}, u32[]{:S(2)}) collective-permute-start(f32[32,1024]{1,0:T(8,128)S(1)} %get-tuple-element.33.refs_4_.first_ref), channel_id=1, source_target_pairs={{0,8},{1,9},{2,10},{3,11},{4,12},{5,13},{6,14},{7,15},{8,0},{9,1},... | collective-permute-start | bytes 393224 | tf_op jit(solution)/shard_map/ppermute | solution.py:52
  72.4 7.1 %collective-permute-start.22 = (f32[2,32,1024]{2,1,0:T(8,128)S(1)}, f32[2,32,1024]{2,1,0:T(8,128)S(1)}, u32[]{:S(2)}, u32[]{:S(2)}) collective-permute-start(f32[2,32,1024]{2,1,0:T(8,128)S(1)} %shard_map.85.refs_0_), channel_id=1, source_target_pairs={{0,64},{1,65},{2,66},{3,67},{4,68},{5,69},{6,70},{7,71},{8,12},{9,... | collective-permute-start | bytes 786440 | tf_op jit(solution)/shard_map/ppermute | solution.py:357
  74.2 8.1 %collective-permute-start.21 = (f32[2,32,1024]{2,1,0:T(8,128)S(1)}, f32[2,32,1024]{2,1,0:T(8,128)S(1)}, u32[]{:S(2)}, u32[]{:S(2)}) collective-permute-start(f32[2,32,1024]{2,1,0:T(8,128)S(1)} %shard_map.85.refs_0_), channel_id=1, source_target_pairs={{0,65},{1,64},{2,67},{3,66},{4,69},{5,68},{6,71},{7,70},{8,14},{9,... | collective-permute-start | bytes 786440 | tf_op jit(solution)/shard_map/ppermute | solution.py:357
  76.0 6.3 %collective-permute-start.20 = (f32[2,32,1024]{2,1,0:T(8,128)S(1)}, f32[2,32,1024]{2,1,0:T(8,128)S(1)}, u32[]{:S(2)}, u32[]{:S(2)}) collective-permute-start(f32[2,32,1024]{2,1,0:T(8,128)S(1)} %shard_map.85.refs_0_), channel_id=1, source_target_pairs={{0,1},{1,0},{2,3},{3,2},{4,5},{5,4},{6,7},{7,6},{8,10},{9,11},{10,... | collective-permute-start | bytes 786440 | tf_op jit(solution)/shard_map/ppermute | solution.py:357
  82.7 5.9 %collective-permute-start.23 = (f32[2,32,1024]{2,1,0:T(8,128)S(1)}, f32[2,32,1024]{2,1,0:T(8,128)S(1)}, u32[]{:S(2)}, u32[]{:S(2)}) collective-permute-start(f32[2,32,1024]{2,1,0:T(8,128)S(1)} %shard_map.87.refs_6_.refs_7_), channel_id=1, source_target_pairs={{0,8},{1,9},{2,10},{3,11},{4,12},{5,13},{6,14},{7,15},{8,0},{9,1},... | collective-permute-start | bytes 786440 | tf_op jit(solution)/shard_map/ppermute | solution.py:52

commit v3 on v2

--- a/solution.py
+++ b/solution.py
@@ -58,6 +58,7 @@
 ANY = pl.BlockSpec(memory_space=pl.ANY)
 SMEM = pl.BlockSpec(memory_space=pltpu.SMEM)
 CHUNK = 256
+BLOCK = 256
 F32 = jnp.float32
 BF16 = jnp.bfloat16
 
@@ -149,22 +150,23 @@
     )(scalars, *arrays)
 
 
-def project_kernel(x_ref, c_ref, e_ref, p_ref, after_ref, z_ref):
-    for slot in range(2):
+def project_kernel(slots, first_ref, second_ref, c_ref, e_ref, p_ref, after_ref, z_ref):
+    turned = (first_ref, second_ref)
+    for n, slot in enumerate(slots):
         p = split(p_ref[slot], 3)
-        w = split(folded(dot(p, x_ref[slot], (1, 1)), 3), 3)
-        z_ref[slot] = folded(dot(w, c_ref[slot], (1, 0)) + dot(p, e_ref[slot], (1, 0)), 3)
-
-
-def project(held, p, after):
-    return pl.pallas_call(
-        project_kernel,
-        out_shape=shape(2, 32, 1024),
-        in_specs=[VMEM] * 4 + [ANY],
+        w = split(folded(dot(p, turned[slot][...], (1, 0)), 3), 3)
+        z_ref[n] = folded(dot(w, c_ref[slot], (1, 0)) + dot(p, e_ref[slot], (1, 0)), 3)
+
+
+def project(turned, held, p, after, slots=(0, 1)):
+    return pl.pallas_call(
+        lambda *refs: project_kernel(slots, *refs),
+        out_shape=shape(len(slots), 32, 1024),
+        in_specs=[VMEM] * 5 + [ANY],
         out_specs=VMEM,
         compiler_params=params(6),
-        cost_estimate=cost(2 * 2 * 96 * 1024 * 2048, 8),
-    )(*held, p, after)
+        cost_estimate=cost(len(slots) * 2 * 96 * 1024 * 2048, 4 * len(slots)),
+    )(*turned, *held[1:], p, after)
 
 
 def gram_schmidt_kernel(slot, p_ref, after_ref, basis_ref, factor_ref):
@@ -221,19 +223,19 @@
     )(scalars, *bases, after)
 
 
-def merge_kernel(slot, x_ref, c_ref, e_ref, after_ref, merged_ref):
+def merge_kernel(slot, x_ref, c_ref, e_ref, after_ref, merged_ref, turned_ref):
     for start in range(0, 1024, CHUNK):
         rows = pl.ds(start, CHUNK)
-        product = dot(x_ref[slot, :, rows], c_ref[slot], (0, 0))
-        merged_ref[rows] = product + e_ref[slot, rows].astype(F32)
+        turned_ref[rows] = x_ref[slot, :, rows].T
+        merged_ref[rows] = dot(turned_ref[rows], c_ref[slot], (1, 0)) + e_ref[slot, rows].astype(F32)
 
 
 def merge(slot, held, after):
     return pl.pallas_call(
         lambda *refs: merge_kernel(slot, *refs),
-        out_shape=pltpu.VMEM((1024, 1024), F32),
+        out_shape=[pltpu.VMEM((1024, 1024), F32), pltpu.VMEM((1024, 512), BF16)],
         in_specs=[VMEM] * 3 + [ANY],
-        out_specs=VMEM,
+        out_specs=[VMEM, VMEM],
         compiler_params=params(6),
         cost_estimate=cost(2 * 512 * 1024 * 1024, 4),
     )(*held, after)
@@ -265,8 +267,8 @@
     for slot, m in enumerate(members(scalars_ref, side)):
         high, low = terms(q_ref[slot], 2)
         right = jnp.concatenate([high, low, high], 0)
-        for n, start in enumerate(range(0, 1024, CHUNK)):
-            block = pl.ds(start, CHUNK)
+        for n, start in enumerate(range(0, 1024, BLOCK)):
+            block = pl.ds(start, BLOCK)
             product = dot(lefts[slot][block], right, (1, 0))
             stage[slot, block] = (merged[slot][block] - product).astype(BF16)
             copy = pltpu.make_async_copy(stage.at[slot, block], error_hbm.at[0, m, block], sems.at[slot, n])
@@ -291,7 +293,7 @@
         out_shape=[shape(1, 4, 1024, 1024, dtype=BF16), shape(2, 8, 1024)],
         in_specs=[SMEM] + [VMEM] * 7,
         out_specs=[HBM, VMEM],
-        scratch_shapes=[pltpu.VMEM((2, 1024, 1024), BF16), pltpu.SemaphoreType.DMA((2, 1024 // CHUNK))],
+        scratch_shapes=[pltpu.VMEM((2, 1024, 1024), BF16), pltpu.SemaphoreType.DMA((2, 1024 // BLOCK))],
         compiler_params=params(8),
         cost_estimate=cost(2 * 2 * 256 * 1024 * 1024, 4),
     )(scalars, *merged, *lefts, *rows, q)
@@ -325,7 +327,7 @@
         scratch_shapes=[
             pltpu.VMEM((4, 8, 1024), BF16),
             pltpu.VMEM((2, 1024, 1024), BF16),
-            pltpu.SemaphoreType.DMA((2, 1024 // CHUNK)),
+            pltpu.SemaphoreType.DMA((2, 1024 // BLOCK)),
             pltpu.SemaphoreType.DMA((2,)),
             pltpu.SemaphoreType.DMA,
         ],
@@ -354,7 +356,7 @@
 
 
 def received(step, value):
-    return [lax.ppermute(value, AXES, step_pairs(step, mask)) for mask in (1, 3, 2)]
+    return [lax.ppermute(value, AXES, step_pairs(step, mask)) for mask in (2, 3, 1)]
 
 
 def on_device(inputs, cotangents, error_buffer, previous_q):
@@ -363,18 +365,18 @@
     *other_held, other = load(0, scalars, arrays)
     *own_held, own = load(1, scalars, arrays)
     total = add([own, other_core(other)])
-    merged = {}
+    merged, turned = {}, {}
     for step in range(3):
         came = received(step, total)
         fill = []
         if step < 2:
-            fill = [merge(slot, other_held if step else own_held, total) for slot in range(2)]
-            merged[1 - step] = fill
-        total = add([total, *came], fill, 1.0 / 128.0 if step == 2 else 1.0)
+            merged[1 - step], turned[1 - step] = zip(*(merge(slot, other_held if step else own_held, total) for slot in range(2)))
+            fill = merged[1 - step]
+        total = add([total, *came], tuple(fill), 1.0 / 128.0 if step == 2 else 1.0)
     mean = total
     other_mean = other_core(mean)
-    own = project(own_held, mean, mean)
-    other = project(other_held, other_mean, own)
+    own = project(turned[1], own_held, mean, mean)
+    other = project(turned[0], other_held, other_mean, own)
     total = add([own, other_core(other)])
     for step in range(3):
         came = received(step, total)

time: 91.9 us -> 91.1 us (level)
  no operation moved by 1% of the time
where the time goes in v3:
time: 91.1 us; the launch traced here: 90.9 us
  Pallas kernels  33.9 us (37%)
  starting transfers between devices  31.4 us (34%)
  waiting for transfers between devices  24.5 us (27%)
  between operations  1.01 us (1%)
    ppermute x18, waiting for transfers between devices, received(): lax.ppermute(value, AXES, step_pairs(step, mask))  23 us
    ppermute x18, starting transfers between devices, received(): lax.ppermute(value, AXES, step_pairs(step, mask))  22.3 us
    pallas_call x2, Pallas kernels, load(): pl.pallas_call(lambda *refs: load_kernel(side, *refs), out_shape=[pltpu.V...  10.2 us
    ppermute x6, starting transfers between devices, other_core(): return lax.ppermute(value, AXES, core_pairs())  9.1 us
    pallas_call x2, Pallas kernels, gram_schmidt(): pl.pallas_call(lambda *refs: gram_schmidt_kernel(slot, *refs), out_shape=...  6.34 us
    pallas_call x4, Pallas kernels, merge(): pl.pallas_call(lambda *refs: merge_kernel(slot, *refs), out_shape=[pltpu....  5.24 us
    pallas_call x1, Pallas kernels, finish_other(): pl.pallas_call(finish_other_kernel, out_shape=[shape(1, 4, 1024, 1024, dt...  3.1 us
    pallas_call x2, Pallas kernels, project(): pl.pallas_call(lambda *refs: project_kernel(slots, *refs), out_shape=shap...  2.92 us
  transfers between devices with their start and end apart: 24, of which 14 were waited for; matrix products, arithmetic and copies ran while one was open for 0% of the time, Pallas kernels for 26%

profile of v3, /device:TPU:1, one launch (start us, length us, event | category | flops | bytes accessed | tf_op | source)
XLA Modules:
  0.0 90.9 jit_solution(7198435052360925965)
XLA Ops:
  0.7 5.1 %shard_map.68 = (bf16[2,512,1024]{2,1,0:T(8,128)(2,1)S(1)}, bf16[2,512,1024]{2,1,0:T(8,128)(2,1)S(1)}, bf16[2,1024,1024]{2,1,0:T(8,128)(2,1)S(1)}, f32[2,32,1024]{2,1,0:T(8,128)S(1)}) custom-call(s32[2]{0:T(128)S(1)} %pad_add_fusion.refs_0_.scalars_ref, bf16[4,512,1024]{2,1,0:T(8,128)(2,1)} %refs_1_.3, bf16[4,512,1024]{2,1,0:T(8,128)(2,1)} %refs_2_.3, ...), custom_call_target="tpu_custom_call" | custom-call | flops 805306368 | bytes 9437184 | tf_op jit(solution)/shard_map/pallas_call | solution.py:137
  5.8 1.5 %collective-permute-start = (f32[2,32,1024]{2,1,0:T(8,128)S(1)}, f32[2,32,1024]{2,1,0:T(8,128)S(1)}, u32[]{:S(2)}, u32[]{:S(2)}) collective-permute-start(f32[2,32,1024]{2,1,0:T(8,128)S(1)} %get-tuple-element.37), channel_id=1, source_target_pairs={{0,8},{1,9},{2,10},{3,11},{4,12},{5,13},{6,14},{7,15},{8,0},{9,1},... | collective-permute-start | bytes 786440 | tf_op jit(solution)/shard_map/ppermute | solution.py:52
  7.3 5.1 %shard_map.67 = (bf16[2,512,1024]{2,1,0:T(8,128)(2,1)S(1)}, bf16[2,512,1024]{2,1,0:T(8,128)(2,1)S(1)}, bf16[2,1024,1024]{2,1,0:T(8,128)(2,1)S(1)}, f32[2,32,1024]{2,1,0:T(8,128)S(1)}) custom-call(s32[2]{0:T(128)S(1)} %pad_add_fusion.refs_0_.scalars_ref, bf16[4,512,1024]{2,1,0:T(8,128)(2,1)} %refs_1_.3, bf16[4,512,1024]{2,1,0:T(8,128)(2,1)} %refs_2_.3, ...), custom_call_target="tpu_custom_call" | custom-call | flops 805306368 | bytes 9437184 | tf_op jit(solution)/shard_map/pallas_call | solution.py:137
  12.5 3.1 %collective-permute-start.1 = (f32[2,32,1024]{2,1,0:T(8,128)S(1)}, f32[2,32,1024]{2,1,0:T(8,128)S(1)}, u32[]{:S(2)}, u32[]{:S(2)}) collective-permute-start(f32[2,32,1024]{2,1,0:T(8,128)S(1)} %shard_map.69.refs_3_.refs_0_), channel_id=1, source_target_pairs={{0,4},{1,5},{2,6},{3,7},{4,0},{5,1},{6,2},{7,3},{8,40},{9,41},{10,... | collective-permute-start | bytes 786440 | tf_op jit(solution)/shard_map/ppermute | solution.py:359
  19.7 2.8 %collective-permute-done.2.refs_2_ = f32[2,32,1024]{2,1,0:T(8,128)S(1)} collective-permute-done((f32[2,32,1024]{2,1,0:T(8,128)S(1)}, f32[2,32,1024]{2,1,0:T(8,128)S(1)}, u32[]{:S(2)}, u32[]{:S(2)}) %collective-permute-start.2) | collective-permute-done | bytes 262176 | tf_op jit(solution)/shard_map/ppermute | solution.py:359
  23.0 3.7 %collective-permute-start.4 = (f32[2,32,1024]{2,1,0:T(8,128)S(1)}, f32[2,32,1024]{2,1,0:T(8,128)S(1)}, u32[]{:S(2)}, u32[]{:S(2)}) collective-permute-start(f32[2,32,1024]{2,1,0:T(8,128)S(1)} %shard_map.72.refs_3_.refs_0_), channel_id=1, source_target_pairs={{0,32},{1,33},{2,34},{3,35},{4,36},{5,37},{6,38},{7,39},{8,72},{9,... | collective-permute-start | bytes 786440 | tf_op jit(solution)/shard_map/ppermute | solution.py:359
  27.4 1.3 %shard_map.74 = (f32[1024,1024]{1,0:T(8,128)S(1)}, bf16[1024,512]{1,0:T(8,128)(2,1)S(1)}) custom-call(bf16[2,512,1024]{2,1,0:T(8,128)(2,1)S(1)} %get-tuple-element.40.refs_0_, bf16[2,512,1024]{2,1,0:T(8,128)(2,1)S(1)} %get-tuple-element.41.refs_1_.refs_2_, bf16[2,1024,1024]{2,1,0:T(8,128)(2,1)S(1)} %get-tuple-element.42.refs_2_.refs_3_, ...), custom_call_target="tpu_custom_call" | custom-call | flops 1073741824 | bytes 4194304 | tf_op jit(solution)/shard_map/pallas_call | solution.py:234
  28.7 1.3 %shard_map.73 = (f32[1024,1024]{1,0:T(8,128)S(1)}, bf16[1024,512]{1,0:T(8,128)(2,1)S(1)}) custom-call(bf16[2,512,1024]{2,1,0:T(8,128)(2,1)S(1)} %get-tuple-element.40.refs_0_, bf16[2,512,1024]{2,1,0:T(8,128)(2,1)S(1)} %get-tuple-element.41.refs_1_.refs_2_, bf16[2,1024,1024]{2,1,0:T(8,128)(2,1)S(1)} %get-tuple-element.42.refs_2_.refs_3_, ...), custom_call_target="tpu_custom_call" | custom-call | flops 1073741824 | bytes 4194304 | tf_op jit(solution)/shard_map/pallas_call | solution.py:234
  30.7 2.8 %collective-permute-done.5.refs_2_ = f32[2,32,1024]{2,1,0:T(8,128)S(1)} collective-permute-done((f32[2,32,1024]{2,1,0:T(8,128)S(1)}, f32[2,32,1024]{2,1,0:T(8,128)S(1)}, u32[]{:S(2)}, u32[]{:S(2)}) %collective-permute-start.5) | collective-permute-done | bytes 262176 | tf_op jit(solution)/shard_map/ppermute | solution.py:359
  34.3 2.2 %collective-permute-start.7 = (f32[2,32,1024]{2,1,0:T(8,128)S(1)}, f32[2,32,1024]{2,1,0:T(8,128)S(1)}, u32[]{:S(2)}, u32[]{:S(2)}) collective-permute-start(f32[2,32,1024]{2,1,0:T(8,128)S(1)} %shard_map.75.refs_0_), channel_id=1, source_target_pairs={{0,64},{1,65},{2,66},{3,67},{4,68},{5,69},{6,70},{7,71},{8,12},{9,... | collective-permute-start | bytes 786440 | tf_op jit(solution)/shard_map/ppermute | solution.py:359
  36.6 1.5 %collective-permute-start.8 = (f32[2,32,1024]{2,1,0:T(8,128)S(1)}, f32[2,32,1024]{2,1,0:T(8,128)S(1)}, u32[]{:S(2)}, u32[]{:S(2)}) collective-permute-start(f32[2,32,1024]{2,1,0:T(8,128)S(1)} %shard_map.75.refs_0_), channel_id=1, source_target_pairs={{0,65},{1,64},{2,67},{3,66},{4,69},{5,68},{6,71},{7,70},{8,14},{9,... | collective-permute-start | bytes 786440 | tf_op jit(solution)/shard_map/ppermute | solution.py:359
  38.0 3.4 %collective-permute-done.7.refs_1_ = f32[2,32,1024]{2,1,0:T(8,128)S(1)} collective-permute-done((f32[2,32,1024]{2,1,0:T(8,128)S(1)}, f32[2,32,1024]{2,1,0:T(8,128)S(1)}, u32[]{:S(2)}, u32[]{:S(2)}) %collective-permute-start.7) | collective-permute-done | bytes 262176 | tf_op jit(solution)/shard_map/ppermute | solution.py:359
  41.4 2.8 %collective-permute-done.8.refs_2_ = f32[2,32,1024]{2,1,0:T(8,128)S(1)} collective-permute-done((f32[2,32,1024]{2,1,0:T(8,128)S(1)}, f32[2,32,1024]{2,1,0:T(8,128)S(1)}, u32[]{:S(2)}, u32[]{:S(2)}) %collective-permute-start.8) | collective-permute-done | bytes 262176 | tf_op jit(solution)/shard_map/ppermute | solution.py:359
  44.3 2.9 %collective-permute-start.10 = (f32[2,32,1024]{2,1,0:T(8,128)S(1)}, f32[2,32,1024]{2,1,0:T(8,128)S(1)}, u32[]{:S(2)}, u32[]{:S(2)}) collective-permute-start(f32[2,32,1024]{2,1,0:T(8,128)S(1)} %shard_map.76.refs_4_.refs_5_.refs_0_), channel_id=1, source_target_pairs={{0,8},{1,9},{2,10},{3,11},{4,12},{5,13},{6,14},{7,15},{8,0},{9,1},... | collective-permute-start | bytes 786440 | tf_op jit(solution)/shard_map/ppermute | solution.py:52
  47.2 1.5 %shard_map.77.refs_5_.refs_0_ = f32[2,32,1024]{2,1,0:T(8,128)S(1)} custom-call(bf16[1024,512]{1,0:T(8,128)(2,1)S(1)} %get-tuple-element.45.refs_0_, bf16[1024,512]{1,0:T(8,128)(2,1)S(1)} %get-tuple-element.46.refs_1_, bf16[2,512,1024]{2,1,0:T(8,128)(2,1)S(1)} %get-tuple-element.34.refs_1_.refs_2_, ...), custom_call_target="tpu_custom_call" | custom-call | flops 805306368 | bytes 8388608 | tf_op jit(solution)/shard_map/pallas_call | solution.py:162
  48.7 1.5 %shard_map.78 = f32[2,32,1024]{2,1,0:T(8,128)S(1)} custom-call(bf16[1024,512]{1,0:T(8,128)(2,1)S(1)} %get-tuple-element.47.refs_0_, bf16[1024,512]{1,0:T(8,128)(2,1)S(1)} %get-tuple-element.48.refs_1_, bf16[2,512,1024]{2,1,0:T(8,128)(2,1)S(1)} %get-tuple-element.41.refs_1_.refs_2_, bf16[2,1024,1024]{2,1,0:T(8,128)(2,1)S(1)} %get-tuple-element.42.refs_2_.refs_3_, ...), custom_call_target="tpu_custom_call" | custom-call | flops 805306368 | bytes 8388608 | tf_op jit(solution)/shard_map/pallas_call | solution.py:162
  50.3 1.5 %collective-permute-done.11.refs_1_ = f32[2,32,1024]{2,1,0:T(8,128)S(1)} collective-permute-done((f32[2,32,1024]{2,1,0:T(8,128)S(1)}, f32[2,32,1024]{2,1,0:T(8,128)S(1)}, u32[]{:S(2)}, u32[]{:S(2)}) %collective-permute-start.11) | collective-permute-done | bytes 262176 | tf_op jit(solution)/shard_map/ppermute | solution.py:52
  51.8 1.8 %collective-permute-start.12 = (f32[2,32,1024]{2,1,0:T(8,128)S(1)}, f32[2,32,1024]{2,1,0:T(8,128)S(1)}, u32[]{:S(2)}, u32[]{:S(2)}) collective-permute-start(f32[2,32,1024]{2,1,0:T(8,128)S(1)} %shard_map.79.refs_1_.refs_0_), channel_id=1, source_target_pairs={{0,4},{1,5},{2,6},{3,7},{4,0},{5,1},{6,2},{7,3},{8,40},{9,41},{10,... | collective-permute-start | bytes 786440 | tf_op jit(solution)/shard_map/ppermute | solution.py:359
  53.6 1.7 %collective-permute-start.13 = (f32[2,32,1024]{2,1,0:T(8,128)S(1)}, f32[2,32,1024]{2,1,0:T(8,128)S(1)}, u32[]{:S(2)}, u32[]{:S(2)}) collective-permute-start(f32[2,32,1024]{2,1,0:T(8,128)S(1)} %shard_map.79.refs_1_.refs_0_), channel_id=1, source_target_pairs={{0,6},{1,7},{2,4},{3,5},{4,2},{5,3},{6,0},{7,1},{8,56},{9,57},{10,... | collective-permute-start | bytes 786440 | tf_op jit(solution)/shard_map/ppermute | solution.py:359
  55.3 3.2 %shard_map.81 = (f32[32,1024]{1,0:T(8,128)S(1)}, f32[32,128]{1,0:T(8,128)S(1)}) custom-call(f32[2,32,1024]{2,1,0:T(8,128)S(1)} %shard_map.76.refs_4_.refs_5_.refs_0_, f32[2,32,1024]{2,1,0:T(8,128)S(1)} %shard_map.79.refs_1_.refs_0_), custom_call_target="tpu_custom_call" | custom-call | flops 4000000 | bytes 8388608 | tf_op jit(solution)/shard_map/pallas_call | solution.py:194
  58.5 3.2 %shard_map.80 = (f32[32,1024]{1,0:T(8,128)S(1)}, f32[32,128]{1,0:T(8,128)S(1)}) custom-call(f32[2,32,1024]{2,1,0:T(8,128)S(1)} %shard_map.76.refs_4_.refs_5_.refs_0_, f32[2,32,1024]{2,1,0:T(8,128)S(1)} %shard_map.79.refs_1_.refs_0_), custom_call_target="tpu_custom_call" | custom-call | flops 4000000 | bytes 8388608 | tf_op jit(solution)/shard_map/pallas_call | solution.py:194
  61.8 1.8 %collective-permute-start.15 = (f32[2,32,1024]{2,1,0:T(8,128)S(1)}, f32[2,32,1024]{2,1,0:T(8,128)S(1)}, u32[]{:S(2)}, u32[]{:S(2)}) collective-permute-start(f32[2,32,1024]{2,1,0:T(8,128)S(1)} %shard_map.82.after_ref.refs_0_), channel_id=1, source_target_pairs={{0,32},{1,33},{2,34},{3,35},{4,36},{5,37},{6,38},{7,39},{8,72},{9,... | collective-permute-start | bytes 786440 | tf_op jit(solution)/shard_map/ppermute | solution.py:359
  63.6 1.4 %collective-permute-start.16 = (f32[2,32,1024]{2,1,0:T(8,128)S(1)}, f32[2,32,1024]{2,1,0:T(8,128)S(1)}, u32[]{:S(2)}, u32[]{:S(2)}) collective-permute-start(f32[2,32,1024]{2,1,0:T(8,128)S(1)} %shard_map.82.after_ref.refs_0_), channel_id=1, source_target_pairs={{0,48},{1,49},{2,50},{3,51},{4,52},{5,53},{6,54},{7,55},{8,73},{9,... | collective-permute-start | bytes 786440 | tf_op jit(solution)/shard_map/ppermute | solution.py:359
  65.0 1.9 %collective-permute-start.19 = (f32[32,1024]{1,0:T(8,128)S(1)}, f32[32,1024]{1,0:T(8,128)S(1)}, u32[]{:S(2)}, u32[]{:S(2)}) collective-permute-start(f32[32,1024]{1,0:T(8,128)S(1)} %get-tuple-element.50.refs_5_.second_ref), channel_id=1, source_target_pairs={{0,8},{1,9},{2,10},{3,11},{4,12},{5,13},{6,14},{7,15},{8,0},{9,1},... | collective-permute-start | bytes 393224 | tf_op jit(solution)/shard_map/ppermute | solution.py:52
  69.5 2.2 %collective-permute-done.16.refs_2_ = f32[2,32,1024]{2,1,0:T(8,128)S(1)} collective-permute-done((f32[2,32,1024]{2,1,0:T(8,128)S(1)}, f32[2,32,1024]{2,1,0:T(8,128)S(1)}, u32[]{:S(2)}, u32[]{:S(2)}) %collective-permute-start.16) | collective-permute-done | bytes 262176 | tf_op jit(solution)/shard_map/ppermute | solution.py:359
  71.8 1.9 %collective-permute-start.20 = (f32[2,32,1024]{2,1,0:T(8,128)S(1)}, f32[2,32,1024]{2,1,0:T(8,128)S(1)}, u32[]{:S(2)}, u32[]{:S(2)}) collective-permute-start(f32[2,32,1024]{2,1,0:T(8,128)S(1)} %shard_map.85.refs_0_), channel_id=1, source_target_pairs={{0,64},{1,65},{2,66},{3,67},{4,68},{5,69},{6,70},{7,71},{8,12},{9,... | collective-permute-start | bytes 786440 | tf_op jit(solution)/shard_map/ppermute | solution.py:359
  73.6 1.8 %collective-permute-start.21 = (f32[2,32,1024]{2,1,0:T(8,128)S(1)}, f32[2,32,1024]{2,1,0:T(8,128)S(1)}, u32[]{:S(2)}, u32[]{:S(2)}) collective-permute-start(f32[2,32,1024]{2,1,0:T(8,128)S(1)} %shard_map.85.refs_0_), channel_id=1, source_target_pairs={{0,65},{1,64},{2,67},{3,66},{4,69},{5,68},{6,71},{7,70},{8,14},{9,... | collective-permute-start | bytes 786440 | tf_op jit(solution)/shard_map/ppermute | solution.py:359
  75.4 3.4 %collective-permute-done.20.refs_1_ = f32[2,32,1024]{2,1,0:T(8,128)S(1)} collective-permute-done((f32[2,32,1024]{2,1,0:T(8,128)S(1)}, f32[2,32,1024]{2,1,0:T(8,128)S(1)}, u32[]{:S(2)}, u32[]{:S(2)}) %collective-permute-start.20) | collective-permute-done | bytes 262176 | tf_op jit(solution)/shard_map/ppermute | solution.py:359
  78.9 2.8 %collective-permute-done.21.refs_2_ = f32[2,32,1024]{2,1,0:T(8,128)S(1)} collective-permute-done((f32[2,32,1024]{2,1,0:T(8,128)S(1)}, f32[2,32,1024]{2,1,0:T(8,128)S(1)}, u32[]{:S(2)}, u32[]{:S(2)}) %collective-permute-start.21) | collective-permute-done | bytes 262176 | tf_op jit(solution)/shard_map/ppermute | solution.py:359
  82.0 2.7 %collective-permute-start.23 = (f32[2,32,1024]{2,1,0:T(8,128)S(1)}, f32[2,32,1024]{2,1,0:T(8,128)S(1)}, u32[]{:S(2)}, u32[]{:S(2)}) collective-permute-start(f32[2,32,1024]{2,1,0:T(8,128)S(1)} %shard_map.87.refs_6_.refs_7_), channel_id=1, source_target_pairs={{0,8},{1,9},{2,10},{3,11},{4,12},{5,13},{6,14},{7,15},{8,0},{9,1},... | collective-permute-start | bytes 786440 | tf_op jit(solution)/shard_map/ppermute | solution.py:52
  84.8 2.9 %shard_map.88 = (bf16[1,4,1024,1024]{3,2,1,0:T(8,128)(2,1)}, f32[2,8,1024]{2,1,0:T(8,128)S(1)}) custom-call(s32[2]{0:T(128)S(1)} %pad_add_fusion.refs_0_.scalars_ref, f32[1024,1024]{1,0:T(8,128)S(1)} %get-tuple-element.38.refs_4_.refs_0_, f32[1024,1024]{1,0:T(8,128)S(1)} %get-tuple-element.39.refs_5_.refs_1_, ...), custom_call_target="tpu_custom_call" | custom-call | flops 1073741824 | bytes 4194304 | tf_op jit(solution)/shard_map/pallas_call | solution.py:291
  87.7 3.1 %shard_map.89 = (bf16[1,4,1024,1024]{3,2,1,0:T(8,128)(2,1)}, bf16[4,8,1024]{2,1,0:T(8,128)(2,1)}, f32[4,32,1024]{2,1,0:T(8,128)}) custom-call(s32[2]{0:T(128)S(1)} %pad_add_fusion.refs_0_.scalars_ref, bf16[1,4,1024,1024]{3,2,1,0:T(8,128)(2,1)} %get-tuple-element.58.earlier_ref, ...), custom_call_target="tpu_custom_call", output_to_operand_aliasing={{0}: (1, {})} | custom-call | flops 1073741824 | bytes 4194304 | tf_op jit(solution)/shard_map/pallas_call | solution.py:322
  (40 shorter events, 10.2 us)
Async XLA Ops:
  5.8 6.6 %collective-permute-start = (f32[2,32,1024]{2,1,0:T(8,128)S(1)}, f32[2,32,1024]{2,1,0:T(8,128)S(1)}, u32[]{:S(2)}, u32[]{:S(2)}) collective-permute-start(f32[2,32,1024]{2,1,0:T(8,128)S(1)} %get-tuple-element.37), channel_id=1, source_target_pairs={{0,8},{1,9},{2,10},{3,11},{4,12},{5,13},{6,14},{7,15},{8,0},{9,1},... | collective-permute-start | bytes 786440 | tf_op jit(solution)/shard_map/ppermute | solution.py:52
  12.5 7.1 %collective-permute-start.1 = (f32[2,32,1024]{2,1,0:T(8,128)S(1)}, f32[2,32,1024]{2,1,0:T(8,128)S(1)}, u32[]{:S(2)}, u32[]{:S(2)}) collective-permute-start(f32[2,32,1024]{2,1,0:T(8,128)S(1)} %shard_map.69.refs_3_.refs_0_), channel_id=1, source_target_pairs={{0,4},{1,5},{2,6},{3,7},{4,0},{5,1},{6,2},{7,3},{8,40},{9,41},{10,... | collective-permute-start | bytes 786440 | tf_op jit(solution)/shard_map/ppermute | solution.py:359
  15.6 6.9 %collective-permute-start.2 = (f32[2,32,1024]{2,1,0:T(8,128)S(1)}, f32[2,32,1024]{2,1,0:T(8,128)S(1)}, u32[]{:S(2)}, u32[]{:S(2)}) collective-permute-start(f32[2,32,1024]{2,1,0:T(8,128)S(1)} %shard_map.69.refs_3_.refs_0_), channel_id=1, source_target_pairs={{0,6},{1,7},{2,4},{3,5},{4,2},{5,3},{6,0},{7,1},{8,56},{9,57},{10,... | collective-permute-start | bytes 786440 | tf_op jit(solution)/shard_map/ppermute | solution.py:359
  16.4 6.5 %collective-permute-start.3 = (f32[2,32,1024]{2,1,0:T(8,128)S(1)}, f32[2,32,1024]{2,1,0:T(8,128)S(1)}, u32[]{:S(2)}, u32[]{:S(2)}) collective-permute-start(f32[2,32,1024]{2,1,0:T(8,128)S(1)} %shard_map.69.refs_3_.refs_0_), channel_id=1, source_target_pairs={{0,2},{1,3},{2,0},{3,1},{4,6},{5,7},{6,4},{7,5},{8,24},{9,25},{10,... | collective-permute-start | bytes 786440 | tf_op jit(solution)/shard_map/ppermute | solution.py:359
  23.0 7.7 %collective-permute-start.4 = (f32[2,32,1024]{2,1,0:T(8,128)S(1)}, f32[2,32,1024]{2,1,0:T(8,128)S(1)}, u32[]{:S(2)}, u32[]{:S(2)}) collective-permute-start(f32[2,32,1024]{2,1,0:T(8,128)S(1)} %shard_map.72.refs_3_.refs_0_), channel_id=1, source_target_pairs={{0,32},{1,33},{2,34},{3,35},{4,36},{5,37},{6,38},{7,39},{8,72},{9,... | collective-permute-start | bytes 786440 | tf_op jit(solution)/shard_map/ppermute | solution.py:359
  26.6 6.9 %collective-permute-start.5 = (f32[2,32,1024]{2,1,0:T(8,128)S(1)}, f32[2,32,1024]{2,1,0:T(8,128)S(1)}, u32[]{:S(2)}, u32[]{:S(2)}) collective-permute-start(f32[2,32,1024]{2,1,0:T(8,128)S(1)} %shard_map.72.refs_3_.refs_0_), channel_id=1, source_target_pairs={{0,48},{1,49},{2,50},{3,51},{4,52},{5,53},{6,54},{7,55},{8,73},{9,... | collective-permute-start | bytes 786440 | tf_op jit(solution)/shard_map/ppermute | solution.py:359
  27.1 7.2 %collective-permute-start.6 = (f32[2,32,1024]{2,1,0:T(8,128)S(1)}, f32[2,32,1024]{2,1,0:T(8,128)S(1)}, u32[]{:S(2)}, u32[]{:S(2)}) collective-permute-start(f32[2,32,1024]{2,1,0:T(8,128)S(1)} %shard_map.72.refs_3_.refs_0_), channel_id=1, source_target_pairs={{0,16},{1,17},{2,18},{3,19},{4,20},{5,21},{6,22},{7,23},{8,9},{9,8... | collective-permute-start | bytes 786440 | tf_op jit(solution)/shard_map/ppermute | solution.py:359
  34.3 7.1 %collective-permute-start.7 = (f32[2,32,1024]{2,1,0:T(8,128)S(1)}, f32[2,32,1024]{2,1,0:T(8,128)S(1)}, u32[]{:S(2)}, u32[]{:S(2)}) collective-permute-start(f32[2,32,1024]{2,1,0:T(8,128)S(1)} %shard_map.75.refs_0_), channel_id=1, source_target_pairs={{0,64},{1,65},{2,66},{3,67},{4,68},{5,69},{6,70},{7,71},{8,12},{9,... | collective-permute-start | bytes 786440 | tf_op jit(solution)/shard_map/ppermute | solution.py:359
  36.6 7.7 %collective-permute-start.8 = (f32[2,32,1024]{2,1,0:T(8,128)S(1)}, f32[2,32,1024]{2,1,0:T(8,128)S(1)}, u32[]{:S(2)}, u32[]{:S(2)}) collective-permute-start(f32[2,32,1024]{2,1,0:T(8,128)S(1)} %shard_map.75.refs_0_), channel_id=1, source_target_pairs={{0,65},{1,64},{2,67},{3,66},{4,69},{5,68},{6,71},{7,70},{8,14},{9,... | collective-permute-start | bytes 786440 | tf_op jit(solution)/shard_map/ppermute | solution.py:359
  38.0 6.3 %collective-permute-start.9 = (f32[2,32,1024]{2,1,0:T(8,128)S(1)}, f32[2,32,1024]{2,1,0:T(8,128)S(1)}, u32[]{:S(2)}, u32[]{:S(2)}) collective-permute-start(f32[2,32,1024]{2,1,0:T(8,128)S(1)} %shard_map.75.refs_0_), channel_id=1, source_target_pairs={{0,1},{1,0},{2,3},{3,2},{4,5},{5,4},{6,7},{7,6},{8,10},{9,11},{10,... | collective-permute-start | bytes 786440 | tf_op jit(solution)/shard_map/ppermute | solution.py:359
  44.3 4.4 %collective-permute-start.10 = (f32[2,32,1024]{2,1,0:T(8,128)S(1)}, f32[2,32,1024]{2,1,0:T(8,128)S(1)}, u32[]{:S(2)}, u32[]{:S(2)}) collective-permute-start(f32[2,32,1024]{2,1,0:T(8,128)S(1)} %shard_map.76.refs_4_.refs_5_.refs_0_), channel_id=1, source_target_pairs={{0,8},{1,9},{2,10},{3,11},{4,12},{5,13},{6,14},{7,15},{8,0},{9,1},... | collective-permute-start | bytes 786440 | tf_op jit(solution)/shard_map/ppermute | solution.py:52
  50.2 1.6 %collective-permute-start.11 = (f32[2,32,1024]{2,1,0:T(8,128)S(1)}, f32[2,32,1024]{2,1,0:T(8,128)S(1)}, u32[]{:S(2)}, u32[]{:S(2)}) collective-permute-start(f32[2,32,1024]{2,1,0:T(8,128)S(1)} %shard_map.78), channel_id=1, source_target_pairs={{0,8},{1,9},{2,10},{3,11},{4,12},{5,13},{6,14},{7,15},{8,0},{9,1},... | collective-permute-start | bytes 786440 | tf_op jit(solution)/shard_map/ppermute | solution.py:52
  51.8 9.9 %collective-permute-start.12 = (f32[2,32,1024]{2,1,0:T(8,128)S(1)}, f32[2,32,1024]{2,1,0:T(8,128)S(1)}, u32[]{:S(2)}, u32[]{:S(2)}) collective-permute-start(f32[2,32,1024]{2,1,0:T(8,128)S(1)} %shard_map.79.refs_1_.refs_0_), channel_id=1, source_target_pairs={{0,4},{1,5},{2,6},{3,7},{4,0},{5,1},{6,2},{7,3},{8,40},{9,41},{10,... | collective-permute-start | bytes 786440 | tf_op jit(solution)/shard_map/ppermute | solution.py:359
  53.6 8.1 %collective-permute-start.13 = (f32[2,32,1024]{2,1,0:T(8,128)S(1)}, f32[2,32,1024]{2,1,0:T(8,128)S(1)}, u32[]{:S(2)}, u32[]{:S(2)}) collective-permute-start(f32[2,32,1024]{2,1,0:T(8,128)S(1)} %shard_map.79.refs_1_.refs_0_), channel_id=1, source_target_pairs={{0,6},{1,7},{2,4},{3,5},{4,2},{5,3},{6,0},{7,1},{8,56},{9,57},{10,... | collective-permute-start | bytes 786440 | tf_op jit(solution)/shard_map/ppermute | solution.py:359
  55.3 6.4 %collective-permute-start.14 = (f32[2,32,1024]{2,1,0:T(8,128)S(1)}, f32[2,32,1024]{2,1,0:T(8,128)S(1)}, u32[]{:S(2)}, u32[]{:S(2)}) collective-permute-start(f32[2,32,1024]{2,1,0:T(8,128)S(1)} %shard_map.79.refs_1_.refs_0_), channel_id=1, source_target_pairs={{0,2},{1,3},{2,0},{3,1},{4,6},{5,7},{6,4},{7,5},{8,24},{9,25},{10,... | collective-permute-start | bytes 786440 | tf_op jit(solution)/shard_map/ppermute | solution.py:359
  61.8 7.7 %collective-permute-start.15 = (f32[2,32,1024]{2,1,0:T(8,128)S(1)}, f32[2,32,1024]{2,1,0:T(8,128)S(1)}, u32[]{:S(2)}, u32[]{:S(2)}) collective-permute-start(f32[2,32,1024]{2,1,0:T(8,128)S(1)} %shard_map.82.after_ref.refs_0_), channel_id=1, source_target_pairs={{0,32},{1,33},{2,34},{3,35},{4,36},{5,37},{6,38},{7,39},{8,72},{9,... | collective-permute-start | bytes 786440 | tf_op jit(solution)/shard_map/ppermute | solution.py:359
  63.6 8.1 %collective-permute-start.16 = (f32[2,32,1024]{2,1,0:T(8,128)S(1)}, f32[2,32,1024]{2,1,0:T(8,128)S(1)}, u32[]{:S(2)}, u32[]{:S(2)}) collective-permute-start(f32[2,32,1024]{2,1,0:T(8,128)S(1)} %shard_map.82.after_ref.refs_0_), channel_id=1, source_target_pairs={{0,48},{1,49},{2,50},{3,51},{4,52},{5,53},{6,54},{7,55},{8,73},{9,... | collective-permute-start | bytes 786440 | tf_op jit(solution)/shard_map/ppermute | solution.py:359
  65.0 6.7 %collective-permute-start.17 = (f32[2,32,1024]{2,1,0:T(8,128)S(1)}, f32[2,32,1024]{2,1,0:T(8,128)S(1)}, u32[]{:S(2)}, u32[]{:S(2)}) collective-permute-start(f32[2,32,1024]{2,1,0:T(8,128)S(1)} %shard_map.82.after_ref.refs_0_), channel_id=1, source_target_pairs={{0,16},{1,17},{2,18},{3,19},{4,20},{5,21},{6,22},{7,23},{8,9},{9,8... | collective-permute-start | bytes 786440 | tf_op jit(solution)/shard_map/ppermute | solution.py:359
  65.0 3.1 %collective-permute-start.19 = (f32[32,1024]{1,0:T(8,128)S(1)}, f32[32,1024]{1,0:T(8,128)S(1)}, u32[]{:S(2)}, u32[]{:S(2)}) collective-permute-start(f32[32,1024]{1,0:T(8,128)S(1)} %get-tuple-element.50.refs_5_.second_ref), channel_id=1, source_target_pairs={{0,8},{1,9},{2,10},{3,11},{4,12},{5,13},{6,14},{7,15},{8,0},{9,1},... | collective-permute-start | bytes 393224 | tf_op jit(solution)/shard_map/ppermute | solution.py:52
  66.9 1.3 %collective-permute-start.18 = (f32[32,1024]{1,0:T(8,128)S(1)}, f32[32,1024]{1,0:T(8,128)S(1)}, u32[]{:S(2)}, u32[]{:S(2)}) collective-permute-start(f32[32,1024]{1,0:T(8,128)S(1)} %get-tuple-element.49.refs_4_.first_ref), channel_id=1, source_target_pairs={{0,8},{1,9},{2,10},{3,11},{4,12},{5,13},{6,14},{7,15},{8,0},{9,1},... | collective-permute-start | bytes 393224 | tf_op jit(solution)/shard_map/ppermute | solution.py:52
  71.8 7.1 %collective-permute-start.20 = (f32[2,32,1024]{2,1,0:T(8,128)S(1)}, f32[2,32,1024]{2,1,0:T(8,128)S(1)}, u32[]{:S(2)}, u32[]{:S(2)}) collective-permute-start(f32[2,32,1024]{2,1,0:T(8,128)S(1)} %shard_map.85.refs_0_), channel_id=1, source_target_pairs={{0,64},{1,65},{2,66},{3,67},{4,68},{5,69},{6,70},{7,71},{8,12},{9,... | collective-permute-start | bytes 786440 | tf_op jit(solution)/shard_map/ppermute | solution.py:359
  73.6 8.1 %collective-permute-start.21 = (f32[2,32,1024]{2,1,0:T(8,128)S(1)}, f32[2,32,1024]{2,1,0:T(8,128)S(1)}, u32[]{:S(2)}, u32[]{:S(2)}) collective-permute-start(f32[2,32,1024]{2,1,0:T(8,128)S(1)} %shard_map.85.refs_0_), channel_id=1, source_target_pairs={{0,65},{1,64},{2,67},{3,66},{4,69},{5,68},{6,71},{7,70},{8,14},{9,... | collective-permute-start | bytes 786440 | tf_op jit(solution)/shard_map/ppermute | solution.py:359
  75.4 6.3 %collective-permute-start.22 = (f32[2,32,1024]{2,1,0:T(8,128)S(1)}, f32[2,32,1024]{2,1,0:T(8,128)S(1)}, u32[]{:S(2)}, u32[]{:S(2)}) collective-permute-start(f32[2,32,1024]{2,1,0:T(8,128)S(1)} %shard_map.85.refs_0_), channel_id=1, source_target_pairs={{0,1},{1,0},{2,3},{3,2},{4,5},{5,4},{6,7},{7,6},{8,10},{9,11},{10,... | collective-permute-start | bytes 786440 | tf_op jit(solution)/shard_map/ppermute | solution.py:359
  82.0 5.6 %collective-permute-start.23 = (f32[2,32,1024]{2,1,0:T(8,128)S(1)}, f32[2,32,1024]{2,1,0:T(8,128)S(1)}, u32[]{:S(2)}, u32[]{:S(2)}) collective-permute-start(f32[2,32,1024]{2,1,0:T(8,128)S(1)} %shard_map.87.refs_6_.refs_7_), channel_id=1, source_target_pairs={{0,8},{1,9},{2,10},{3,11},{4,12},{5,13},{6,14},{7,15},{8,0},{9,1},... | collective-permute-start | bytes 786440 | tf_op jit(solution)/shard_map/ppermute | solution.py:52
